TPU v7x, 32 devices: a whole 2x2x4 slice. The times are simulated.
32 devices in a mesh: dp: 8 (over z, core), expert: 4 (over y, x).
Axes of the slice: x: 2, y: 2, z: 4, core: 2. Of those that a mesh axis runs over, the one named last changes fastest.
Arguments:
- tokens: bfloat16 [2048, 2048], P(('dp', 'expert')), parts along dimension 0, may hold values from -6 to 6
- router_weight: bfloat16 [2048, 4], replicated, may hold values from -0.125 to 0.125
- gate_weight: bfloat16 [4, 2048, 768], P('expert'), may hold values from -0.125 to 0.125
- up_weight: bfloat16 [4, 2048, 768], P('expert'), may hold values from -0.125 to 0.125
- down_weight: bfloat16 [4, 768, 2048], P('expert'), may hold values from -0.21875 to 0.21875
- routing: int32 [2048, 4], P(('dp', 'expert')), parts along dimension 0, may hold values from 0 to 3, as said below
- priority: int32 [32, 256], P(('dp', 'expert')), parts along dimension 0, may hold values from 0 to 255, each once within a row
- hot_list: int32 [16], P('dp'), parts along dimension 0, may hold values from 0 to 3, as said below
Outputs:
- mixed: bfloat16 [2048, 2048], P(('dp', 'expert')), parts along dimension 0
There are 8 independent parts, one for each index of `dp`. A program takes and returns all parts, laid end to end along the dimension named above; an argument that names none is the same for every part. Nothing has to cross between parts.
Inputs may be any that keep to these rules, and one draw needn't show every extreme that they name: `routing`: each token names 4 different experts. `priority`: each row is a permutation. `hot_list`: 2 different experts.
All inputs are finite; a program needn't handle non-finite values.
Results may differ from a plain program's by a relative error of at most 0.0085.
Values may be sent and summed in bfloat16 or wider, within the bound.
No kernel may reach another device: no remote copies, remote signals or barrier semaphores. Data moves between devices by JAX's collectives and lax.ppermute only.
A program may use at most 64 MiB of HBM per device.

v0:
```python
import jax
import jax.numpy as jnp
from jax import lax
from jax.sharding import PartitionSpec as P


def expert_swiglu(inputs, gate_mat, up_mat, down_mat):
    gate_part = jnp.dot(inputs, gate_mat, preferred_element_type=jnp.float32)
    up_part = jnp.dot(inputs, up_mat, preferred_element_type=jnp.float32)
    hidden = (jax.nn.silu(gate_part) * up_part).astype(jnp.bfloat16)
    return jnp.dot(hidden, down_mat, preferred_element_type=jnp.float32).astype(jnp.bfloat16)


def shards(tokens, router_weight, gate_weight, up_weight, down_weight, routing, priority, hot_list):
    devices_n = lax.axis_size("expert")
    tok_count, width = tokens.shape
    top_count = routing.shape[1]
    slot_count = tok_count * top_count
    capacity = min(tok_count, 3 * slot_count // (2 * devices_n))
    logits = jnp.dot(tokens, router_weight, preferred_element_type=jnp.float32)
    chosen = jnp.take_along_axis(logits, routing, axis=1)
    sigmas = jax.nn.sigmoid(chosen)
    weights = sigmas / jnp.sum(sigmas, axis=1, keepdims=True)
    hot_flag = jnp.any(routing[:, :, None] == hot_list[None, None, :], axis=2)
    slot_expert = routing.reshape(-1)
    slot_order = priority[0]
    same_expert = slot_expert[:, None] == slot_expert[None, :]
    earlier = slot_order[None, :] < slot_order[:, None]
    ranks = jnp.sum((same_expert & earlier).astype(jnp.int32), axis=1)
    sending = jnp.logical_not(hot_flag.reshape(-1)) & (ranks < capacity)
    cell_index = slot_expert * capacity + ranks
    cell_count = devices_n * capacity
    cells = lax.broadcasted_iota(jnp.int32, (cell_count, slot_count), 0)
    placed = (cells == cell_index[None, :]) & sending[None, :]
    dispatch = jnp.sum(
        placed.reshape(cell_count, tok_count, top_count).astype(jnp.float32), axis=2
    ).astype(jnp.bfloat16)
    outbound = jnp.dot(dispatch, tokens, preferred_element_type=jnp.float32).astype(jnp.bfloat16)
    outbound = outbound.reshape(devices_n, capacity, width)
    received = lax.all_to_all(outbound, "expert", split_axis=0, concat_axis=0, tiled=True)
    flat_rows = received.reshape(-1, width)
    answer = expert_swiglu(flat_rows, gate_weight[0], up_weight[0], down_weight[0]).reshape(
        received.shape
    )
    returned = lax.all_to_all(answer, "expert", split_axis=0, concat_axis=0, tiled=True)
    returned_flat = returned.reshape(cell_count, width)
    safe_cell = jnp.where(sending, cell_index, 0)
    slot_answer = jnp.take(returned_flat, safe_cell, axis=0).reshape(tok_count, top_count, width)
    slot_weight = jnp.where(sending.reshape(tok_count, top_count), weights, 0.0)
    mixed = jnp.sum(slot_weight[:, :, None] * slot_answer.astype(jnp.float32), axis=1)
    owners = lax.broadcasted_iota(jnp.int32, (devices_n, tok_count, top_count), 0)
    picked = (routing[None, :, :] == owners) & hot_flag[None, :, :]
    asked = jnp.any(picked, axis=2)
    outgoing = jnp.where(asked[:, :, None], tokens[None, :, :], jnp.zeros((), jnp.bfloat16))
    received = lax.all_to_all(outgoing, "expert", split_axis=0, concat_axis=0, tiled=True)
    flat_rows = received.reshape(-1, width)
    answer = expert_swiglu(flat_rows, gate_weight[0], up_weight[0], down_weight[0]).reshape(
        received.shape
    )
    answers = lax.all_to_all(answer, "expert", split_axis=0, concat_axis=0, tiled=True)
    hot_answers = jnp.take(answers, hot_list, axis=0)
    hot_share = jnp.sum(
        jnp.where(routing[None, :, :] == hot_list[:, None, None], weights[None, :, :], 0.0), axis=2
    )
    mixed = mixed + jnp.sum(hot_share[:, :, None] * hot_answers.astype(jnp.float32), axis=0)
    return mixed.astype(jnp.bfloat16)


def solution(mesh):
    return jax.shard_map(
        shards,
        mesh=mesh,
        in_specs=(
            P(("dp", "expert"), None),
            P(),
            P("expert", None, None),
            P("expert", None, None),
            P("expert", None, None),
            P(("dp", "expert"), None),
            P(("dp", "expert"), None),
            P("dp"),
        ),
        out_specs=P(("dp", "expert"), None),
        check_vma=False,
    )
```

profile of v0, /device:TPU:0, one launch (start us, length us, event | category | flops | bytes accessed | tf_op | source)
XLA Modules:
  0.0 83.9 jit_solution(11440994689456043016)
XLA Ops:
  0.0 0.9 %copy.28 = s32[64,4]{1,0:T(8,128)S(1)} copy(s32[64,4]{0,1:T(4,128)} %param.13) | data formatting | bytes 2048 | tf_op args[5]
  1.1 1.0 %convert_reduce_fusion.1 = s32[256]{0:T(256)S(1)} fusion(s32[256]{0:T(256)} %bitcast.56, s32[256]{0:T(256)S(1)} %eq.61), kind=kLoop, calls=%fused_computation.30 | loop fusion | flops 327424 | bytes 3072 | tf_op jit(solution)/shard_map/reduce_sum | solution.py:29
  2.0 0.1 reduce_sum.59
  2.2 0.8 compare_reduce_fusion
  3.0 0.7 compare_and_fusion.1
  3.7 0.1 convert_reduce_fusion
  3.8 2.4 %convolution_convert_fusion = bf16[256,2048]{1,0:T(8,128)(2,1)} fusion(bf16[64,2048]{1,0:T(8,128)(2,1)} %param.8, bf16[256,64]{0,1:T(8,128)(2,1)S(1)} %convert_reduce_fusion), kind=kOutput, calls=%fused_computation.17 | convolution fusion | flops 67633152 | bytes 1343488 | tf_op jit(solution)/shard_map/dot_general | solution.py:38
  6.3 5.2 %all-to-all-start = ((bf16[4,64,2048]{2,1,0:T(8,128)(2,1)}), bf16[4,64,2048]{2,1,0:T(8,128)(2,1)}, u32[]{:S(2)}, u32[]{:S(2)}) async-start(bf16[4,64,2048]{2,1,0:T(8,128)(2,1)} %bitcast.52), calls=%async_computation | async-start | bytes 2097152 | tf_op jit(solution)/shard_map/all_to_all | solution.py:40
  11.5 0.1 copy.35
  11.6 0.1 not.24
  11.8 0.1 mul.53
  12.1 0.2 fusion.44
  12.3 2.4 %gather_fusion.2 = f32[256]{0:T(256)S(1)} fusion(f32[64,4]{0,1:T(4,128)S(1)} %fusion.44, s32[256]{0:T(256)S(1)} %reshape.199), kind=kCustom, calls=%fused_computation.2 | custom fusion | bytes 4096 | tf_op jit(solution)/shard_map/jit(take_along_axis)/gather | solution.py:21
  15.1 0.1 copy.34
  15.3 1.1 %broadcast_select_fusion = bf16[4,64,2048]{2,1,0:T(8,128)(2,1)} fusion(pred[4,64]{1,0:T(4,128)(4,1)S(1)} %fusion.39, bf16[64,2048]{1,0:T(8,128)(2,1)S(1)} %copy-done.1), kind=kLoop, calls=%fused_computation.24 | loop fusion | flops 524288 | bytes 1310976 | tf_op jit(solution)/shard_map/jit(_where)/select_n | solution.py:54
  16.4 9.3 %all-to-all-done = bf16[4,64,2048]{2,1,0:T(8,128)(2,1)} async-done(((bf16[4,64,2048]{2,1,0:T(8,128)(2,1)}), bf16[4,64,2048]{2,1,0:T(8,128)(2,1)}, u32[]{:S(2)}, u32[]{:S(2)}) %all-to-all-start) | async-done | bytes 1048608 | tf_op jit(solution)/shard_map/all_to_all | solution.py:40
  25.7 4.3 %all-to-all-start.2 = ((bf16[4,64,2048]{2,1,0:T(8,128)(2,1)}), bf16[4,64,2048]{2,1,0:T(8,128)(2,1)}, u32[]{:S(2)}, u32[]{:S(2)}) async-start(bf16[4,64,2048]{2,1,0:T(8,128)(2,1)} %broadcast_select_fusion), calls=%async_computation.2 | async-start | bytes 2097152 | tf_op jit(solution)/shard_map/all_to_all | solution.py:55
  30.0 4.1 %fusion.10 = f32[256,768]{1,0:T(8,128)} fusion(bf16[256,2048]{1,0:T(8,128)(2,1)} %bitcast.3, bf16[1,2048,768]{2,1,0:T(8,128)(2,1)} %param.10), kind=kOutput, calls=%fused_computation.13 | convolution fusion | flops 805306368 | bytes 4980736 | tf_op jit(solution)/shard_map/dot_general | solution.py:8
  34.1 5.5 %fusion.12 = bf16[256,2048]{1,0:T(8,128)(2,1)} fusion(bf16[1,768,2048]{2,1,0:T(8,128)(2,1)S(1)} %copy-done, bf16[256,2048]{1,0:T(8,128)(2,1)} %bitcast.3, bf16[1,2048,768]{2,1,0:T(8,128)(2,1)} %param.11, f32[256,768]{1,0:T(8,128)} %fusion.10), kind=kOutput, calls=%fused_computation.15 | convolution fusion | flops 1612316672 | bytes 9175040 | tf_op jit(solution)/shard_map/dot_general | solution.py:11
  39.6 3.8 %all-to-all-done.2 = bf16[4,64,2048]{2,1,0:T(8,128)(2,1)} async-done(((bf16[4,64,2048]{2,1,0:T(8,128)(2,1)}), bf16[4,64,2048]{2,1,0:T(8,128)(2,1)}, u32[]{:S(2)}, u32[]{:S(2)}) %all-to-all-start.2) | async-done | bytes 1048608 | tf_op jit(solution)/shard_map/all_to_all | solution.py:55
  43.4 4.3 %all-to-all-start.1 = ((bf16[4,64,2048]{2,1,0:T(8,128)(2,1)}), bf16[4,64,2048]{2,1,0:T(8,128)(2,1)}, u32[]{:S(2)}, u32[]{:S(2)}) async-start(bf16[4,64,2048]{2,1,0:T(8,128)(2,1)} %bitcast.54), calls=%async_computation.1 | async-start | bytes 2097152 | tf_op jit(solution)/shard_map/all_to_all | solution.py:45
  47.7 4.1 %fusion.8 = f32[256,768]{1,0:T(8,128)} fusion(bf16[256,2048]{1,0:T(8,128)(2,1)} %bitcast.11, bf16[1,2048,768]{2,1,0:T(8,128)(2,1)} %param.10), kind=kOutput, calls=%fused_computation.11 | convolution fusion | flops 805306368 | bytes 4980736 | tf_op jit(solution)/shard_map/dot_general | solution.py:8
  51.7 5.6 %fusion.15 = bf16[256,2048]{1,0:T(8,128)(2,1)} fusion(bf16[1,768,2048]{2,1,0:T(8,128)(2,1)S(1)} %copy-done, bf16[256,2048]{1,0:T(8,128)(2,1)} %bitcast.11, bf16[1,2048,768]{2,1,0:T(8,128)(2,1)} %param.11, f32[256,768]{1,0:T(8,128)} %fusion.8), kind=kOutput, calls=%fused_computation.16 | convolution fusion | flops 1612316672 | bytes 9175040 | tf_op jit(solution)/shard_map/dot_general | solution.py:11
  57.3 3.5 %all-to-all-done.1 = bf16[4,64,2048]{2,1,0:T(8,128)(2,1)} async-done(((bf16[4,64,2048]{2,1,0:T(8,128)(2,1)}), bf16[4,64,2048]{2,1,0:T(8,128)(2,1)}, u32[]{:S(2)}, u32[]{:S(2)}) %all-to-all-start.1) | async-done | bytes 1048608 | tf_op jit(solution)/shard_map/all_to_all | solution.py:45
  60.8 4.4 %all-to-all-start.3 = ((bf16[4,64,2048]{2,1,0:T(8,128)(2,1)}), bf16[4,64,2048]{2,1,0:T(8,128)(2,1)}, u32[]{:S(2)}, u32[]{:S(2)}) async-start(bf16[4,64,2048]{2,1,0:T(8,128)(2,1)} %bitcast.53), calls=%async_computation.3 | async-start | bytes 2097152 | tf_op jit(solution)/shard_map/all_to_all | solution.py:60
  65.4 4.7 %gather_fusion = bf16[256,2048]{1,0:T(8,128)(2,1)} fusion(bf16[256,2048]{1,0:T(8,128)(2,1)} %bitcast.8, s32[1024]{0:T(1024)S(1)} %pad_clamp_fusion.1), kind=kCustom, calls=%fused_computation | custom fusion | bytes 2098176 | tf_op jit(solution)/shard_map/jit(_take)/gather | solution.py:48
  70.1 2.3 %gather.16 = bf16[64,4,2048]{2,1,0:T(4,128)(2,1)} reshape(bf16[256,2048]{1,0:T(8,128)(2,1)} %gather_fusion) | data formatting | bytes 2097152 | tf_op jit(solution)/shard_map/jit(_take)/gather | solution.py:48
  72.3 4.6 %multiply_reduce_fusion = f32[64,2048]{1,0:T(8,128)} fusion(bf16[64,4,2048]{2,1,0:T(4,128)(2,1)} %gather.16, f32[64,4]{1,0:T(8,128)S(1)} %copy.32, pred[64,4]{1,0:T(8,128)(4,1)S(1)} %copy.34), kind=kLoop, calls=%fused_computation.18 | loop fusion | flops 1966080 | bytes 1574144 | tf_op jit(solution)/shard_map/reduce_sum | solution.py:50
  77.0 1.2 %all-to-all-done.3 = bf16[4,64,2048]{2,1,0:T(8,128)(2,1)} async-done(((bf16[4,64,2048]{2,1,0:T(8,128)(2,1)}), bf16[4,64,2048]{2,1,0:T(8,128)(2,1)}, u32[]{:S(2)}, u32[]{:S(2)}) %all-to-all-start.3) | async-done | bytes 1048608 | tf_op jit(solution)/shard_map/all_to_all | solution.py:60
  78.2 2.6 %gather_fusion.1 = bf16[2,64,2048]{2,1,0:T(8,128)(2,1)} fusion(bf16[4,64,2048]{2,1,0:T(8,128)(2,1)} %all-to-all-done.3, s32[1024]{0:T(1024)S(1)} %pad_clamp_fusion), kind=kCustom, calls=%fused_computation.1 | custom fusion | bytes 1048584 | tf_op jit(solution)/shard_map/jit(_take)/gather | solution.py:61
  80.8 1.3 %multiply_reduce_fusion.1 = f32[64,2048]{1,0:T(8,128)S(1)} fusion(bf16[2,64,2048]{2,1,0:T(8,128)(2,1)} %gather_fusion.1, f32[2,64]{1,0:T(2,128)S(1)} %select_reduce_fusion, pred[2]{0:T(512)(128)(4,1)S(1)} %compare_and_fusion), kind=kLoop, calls=%fused_computation.23 | loop fusion | flops 917504 | bytes 1049090 | tf_op jit(solution)/shard_map/reduce_sum | solution.py:65
  82.1 1.8 %add_convert_fusion = bf16[64,2048]{1,0:T(8,128)(2,1)} fusion(f32[64,2048]{1,0:T(8,128)} %multiply_reduce_fusion, f32[64,2048]{1,0:T(8,128)S(1)} %multiply_reduce_fusion.1), kind=kLoop, calls=%fused_computation.25 | loop fusion | flops 262144 | bytes 1310720 | tf_op jit(solution)/shard_map/convert_element_type | solution.py:66
  (29 shorter events, 1.0 us)
Async XLA Ops:
  0.0 34.1 %copy-start = (bf16[1,768,2048]{2,1,0:T(8,128)(2,1)S(1)}, bf16[1,768,2048]{2,1,0:T(8,128)(2,1)}, u32[]{:S(2)}) copy-start(bf16[1,768,2048]{2,1,0:T(8,128)(2,1)} %param.12) | copy-start | bytes 9437188
  0.0 11.4 %copy-start.2 = (s32[64,4]{0,1:T(4,128)S(1)}, s32[64,4]{0,1:T(4,128)}, u32[]{:S(2)}) copy-start(s32[64,4]{0,1:T(4,128)} %param.13) | copy-start | bytes 3076
  0.0 11.5 %copy-start.4 = (s32[2]{0:T(128)S(1)}, s32[2]{0:T(128)}, u32[]{:S(2)}) copy-start(s32[2]{0:T(128)} %param.15) | copy-start | bytes 28
  0.0 12.1 %copy-start.1 = (bf16[64,2048]{1,0:T(8,128)(2,1)S(1)}, bf16[64,2048]{1,0:T(8,128)(2,1)}, u32[]{:S(2)}) copy-start(bf16[64,2048]{1,0:T(8,128)(2,1)} %param.8) | copy-start | bytes 786436
  0.0 12.1 %copy-start.3 = (bf16[2048,4]{0,1:T(4,128)(2,1)S(1)}, bf16[2048,4]{0,1:T(4,128)(2,1)}, u32[]{:S(2)}) copy-start(bf16[2048,4]{0,1:T(4,128)(2,1)} %param.9) | copy-start | bytes 49156
  6.3 19.4 %all-to-all-start = ((bf16[4,64,2048]{2,1,0:T(8,128)(2,1)}), bf16[4,64,2048]{2,1,0:T(8,128)(2,1)}, u32[]{:S(2)}, u32[]{:S(2)}) async-start(bf16[4,64,2048]{2,1,0:T(8,128)(2,1)} %bitcast.52), calls=%async_computation | async-start | bytes 2097152 | tf_op jit(solution)/shard_map/all_to_all | solution.py:40
  25.7 17.7 %all-to-all-start.2 = ((bf16[4,64,2048]{2,1,0:T(8,128)(2,1)}), bf16[4,64,2048]{2,1,0:T(8,128)(2,1)}, u32[]{:S(2)}, u32[]{:S(2)}) async-start(bf16[4,64,2048]{2,1,0:T(8,128)(2,1)} %broadcast_select_fusion), calls=%async_computation.2 | async-start | bytes 2097152 | tf_op jit(solution)/shard_map/all_to_all | solution.py:55
  43.4 17.4 %all-to-all-start.1 = ((bf16[4,64,2048]{2,1,0:T(8,128)(2,1)}), bf16[4,64,2048]{2,1,0:T(8,128)(2,1)}, u32[]{:S(2)}, u32[]{:S(2)}) async-start(bf16[4,64,2048]{2,1,0:T(8,128)(2,1)} %bitcast.54), calls=%async_computation.1 | async-start | bytes 2097152 | tf_op jit(solution)/shard_map/all_to_all | solution.py:45
  60.8 17.4 %all-to-all-start.3 = ((bf16[4,64,2048]{2,1,0:T(8,128)(2,1)}), bf16[4,64,2048]{2,1,0:T(8,128)(2,1)}, u32[]{:S(2)}, u32[]{:S(2)}) async-start(bf16[4,64,2048]{2,1,0:T(8,128)(2,1)} %bitcast.53), calls=%async_computation.3 | async-start | bytes 2097152 | tf_op jit(solution)/shard_map/all_to_all | solution.py:60
where the time goes:
time: 84.6 us; the launch traced here: 83.9 us
  matrix products  21.8 us (26%)
  starting transfers between devices  18.1 us (21%)
  waiting for transfers between devices  17.9 us (21%)
  local copies, waits for them, and re-layouts  14.2 us (17%)
  other arithmetic  11.6 us (14%)
    dot_general x2, matrix products, expert_swiglu(): jnp.dot(hidden, down_mat, preferred_element_type=jnp.float32)  11.1 us
    all_to_all x1, waiting for transfers between devices, shards(): lax.all_to_all(outbound, 'expert', split_axis=0, concat_axis=0, tiled=True)  9.32 us
    all_to_all x2, starting transfers between devices, shards(): lax.all_to_all(answer, 'expert', split_axis=0, concat_axis=0, tiled=True)  8.7 us
    dot_general x2, matrix products, expert_swiglu(): gate_part = jnp.dot(inputs, gate_mat, preferred_element_type=jnp.float32)  8.14 us
    gather x2, local copies, waits for them, and re-layouts, shards(): jnp.take(returned_flat, safe_cell, axis=0)  6.96 us
    all_to_all x1, starting transfers between devices, shards(): lax.all_to_all(outbound, 'expert', split_axis=0, concat_axis=0, tiled=True)  5.17 us
    all_to_all x2, waiting for transfers between devices, shards(): lax.all_to_all(answer, 'expert', split_axis=0, concat_axis=0, tiled=True)  4.75 us
    reduce_sum x1, other arithmetic, shards(): jnp.sum(slot_weight[:, :, None] * slot_answer.astype(jnp.float32), axis=1)  4.63 us
  transfers between devices with their start and end apart: 4, of which 4 were waited for; matrix products, arithmetic and copies ran while one was open for 43% of the time, Pallas kernels for 0%

commit v1 on v0

v1 whole, which is shorter than its diff:
```python
import functools

import jax
import jax.numpy as jnp
from jax import lax
from jax.experimental import pallas as pl
from jax.experimental.pallas import tpu as pltpu
from jax.sharding import PartitionSpec as P

VMEM = pl.BlockSpec(memory_space=pltpu.VMEM)
SMEM = pl.BlockSpec(memory_space=pltpu.SMEM)
ROOM = 32 << 20


def share_kernel(capacity, peers, me_ref, hot_ref, tokens_ref, router_ref, routing_ref, priority_ref, share_ref):
    logits = jnp.dot(tokens_ref[...], router_ref[...], preferred_element_type=jnp.float32)
    sigmas = 1.0 / (1.0 + jnp.exp(-logits))
    routing = routing_ref[...]
    rows, top = routing.shape
    slots = rows * top
    experts = logits.shape[1]
    expert_at = lax.broadcasted_iota(jnp.int32, (rows, experts), 1)
    choice = lax.broadcasted_iota(jnp.int32, (rows, slots), 1) - top * lax.broadcasted_iota(
        jnp.int32, (rows, slots), 0
    )
    priority = jnp.broadcast_to(priority_ref[...], (rows, slots))
    columns = [routing[:, k : k + 1] for k in range(top)]
    slot_priority = [
        jnp.sum(jnp.where(choice == k, priority, 0), axis=1, keepdims=True) for k in range(top)
    ]
    slot_expert = jnp.zeros((1, slots), jnp.int32)
    total = jnp.zeros((rows, 1), jnp.float32)
    for k in range(top):
        slot_expert += jnp.sum(jnp.where(choice == k, columns[k], 0), axis=0, keepdims=True)
        total += jnp.sum(jnp.where(expert_at == columns[k], sigmas, 0.0), axis=1, keepdims=True)
    lane = lax.broadcasted_iota(jnp.int32, share_ref.shape, 1)
    share = jnp.zeros(share_ref.shape, jnp.float32)
    for d, peer in enumerate(peers):
        expert = peer(me_ref[0])
        here = jnp.zeros((rows, 1), jnp.int32)
        mine = jnp.zeros((rows, 1), jnp.int32)
        for k in range(top):
            at = columns[k] == expert
            here += at.astype(jnp.int32)
            mine += jnp.where(at, slot_priority[k], 0)
        rank = jnp.sum(
            ((slot_expert == expert) & (priority < mine)).astype(jnp.int32), axis=1, keepdims=True
        )
        hot = jnp.int32(0)
        for h in range(hot_ref.shape[0]):
            hot += (hot_ref[h] == expert).astype(jnp.int32)
        keeping = (here > 0) & ((rank < capacity) | (hot > 0))
        sigma = jnp.sum(jnp.where(expert_at == expert, sigmas, 0.0), axis=1, keepdims=True)
        share = jnp.where(lane == d, jnp.where(keeping, sigma / total, 0.0), share)
    share_ref[...] = share


def expert_kernel(inputs_ref, gate_ref, up_ref, down_ref, answer_ref):
    gate_part = jnp.dot(inputs_ref[...], gate_ref[0], preferred_element_type=jnp.float32)
    up_part = jnp.dot(inputs_ref[...], up_ref[0], preferred_element_type=jnp.float32)
    hidden = (gate_part / (1.0 + jnp.exp(-gate_part)) * up_part).astype(jnp.bfloat16)
    answer_ref[...] = jnp.dot(hidden, down_ref[0], preferred_element_type=jnp.float32).astype(
        answer_ref.dtype
    )


def mix_kernel(share_ref, *refs):
    *answers, mixed_ref = refs
    total = share_ref[:, 0:1] * answers[0][...].astype(jnp.float32)
    for d in range(1, len(answers)):
        total += share_ref[:, d : d + 1] * answers[d][...].astype(jnp.float32)
    mixed_ref[...] = total.astype(mixed_ref.dtype)


def call(kernel, shape, dtype, operands, specs=None, cost=None):
    return pl.pallas_call(
        kernel,
        out_shape=jax.ShapeDtypeStruct(shape, dtype),
        in_specs=specs or [VMEM] * len(operands),
        out_specs=VMEM,
        compiler_params=pltpu.CompilerParams(vmem_limit_bytes=ROOM),
        cost_estimate=cost,
    )(*operands)


def shards(tokens, router_weight, gate_weight, up_weight, down_weight, routing, priority, hot_list):
    devices_n = lax.axis_size("expert")
    tok_count, width = tokens.shape
    hidden_n = gate_weight.shape[2]
    slot_count = tok_count * routing.shape[1]
    capacity = min(tok_count, 3 * slot_count // (2 * devices_n))
    me = lax.axis_index("expert").astype(jnp.int32).reshape(1)
    if devices_n & (devices_n - 1) == 0:
        paths = [(lambda i, d=d: i ^ d) for d in range(devices_n)]
        backs = paths
    else:
        paths = [(lambda i, d=d: (i + d) % devices_n) for d in range(devices_n)]
        backs = [(lambda i, d=d: (i + devices_n - d) % devices_n) for d in range(devices_n)]

    def send(array, path):
        return lax.ppermute(array, "expert", [(i, path(i)) for i in range(devices_n)])

    def answer(rows):
        cost = pl.CostEstimate(
            flops=6 * rows.shape[0] * width * hidden_n, bytes_accessed=6 * width * hidden_n, transcendentals=0
        )
        return call(expert_kernel, rows.shape, rows.dtype, (rows, gate_weight, up_weight, down_weight), cost=cost)

    arrived = [send(tokens, paths[d]) for d in range(1, devices_n)]
    share = call(
        functools.partial(share_kernel, capacity, paths),
        (tok_count, 128),
        jnp.float32,
        (me, hot_list, tokens, router_weight, routing, priority),
        [SMEM, SMEM] + [VMEM] * 4,
    )
    answers = [answer(tokens)]
    for d in range(1, devices_n):
        answers.append(send(answer(arrived[d - 1]), backs[d]))
    return call(mix_kernel, tokens.shape, tokens.dtype, (share, *answers))


def solution(mesh):
    return jax.shard_map(
        shards,
        mesh=mesh,
        in_specs=(
            P(("dp", "expert"), None),
            P(),
            P("expert", None, None),
            P("expert", None, None),
            P("expert", None, None),
            P(("dp", "expert"), None),
            P(("dp", "expert"), None),
            P("dp"),
        ),
        out_specs=P(("dp", "expert"), None),
        check_vma=False,
    )
```

time: 84.6 us -> 39.5 us (0.47)
  matrix products: 21.8 us -> 0 us
  Pallas kernels: 0 us -> 13.5 us
  waiting for transfers between devices: 17.9 us -> 5.83 us
  other arithmetic: 11.6 us -> 0 us
  starting transfers between devices: 18.1 us -> 8.11 us
  local copies, waits for them, and re-layouts: 14.2 us -> 11.6 us
    dot_general x6 -> x0, matrix products: 21.8 us -> none  [the longest x2 11.1 us: expert_swiglu(): jnp.dot(hidden, down_mat, preferred_element_type=jnp.float32)]
    all_to_all x4 -> x0, starting transfers between devices: 18.1 us -> none  [the longest x2 8.7 us: shards(): lax.all_to_all(answer, 'expert', split_axis=0, concat_axis=0, tiled=True)]
    all_to_all x4 -> x0, waiting for transfers between devices: 17.9 us -> none  [the longest x1 9.32 us: shards(): lax.all_to_all(outbound, 'expert', split_axis=0, concat_axis=0, tiled=True)]
    pallas_call x0 -> x6, Pallas kernels: none -> 13.5 us  [call(): pl.pallas_call(kernel, out_shape=jax.ShapeDtypeStruct(shape, dtype), in_s...]
    gather x8 -> x0, local copies, waits for them, and re-layouts: 12.4 us -> none  [the longest x2 6.96 us: shards(): jnp.take(returned_flat, safe_cell, axis=0)]
    unnamed x11 -> x26, local copies, waits for them, and re-layouts: 0.94 us -> 11.6 us
    ppermute x0 -> x6, starting transfers between devices: none -> 8.11 us  [send(): lax.ppermute(array, 'expert', [(i, path(i)) for i in range(devices_n)])]
    reduce_sum x6 -> x0, other arithmetic: 7.12 us -> none  [the longest x1 4.63 us: shards(): jnp.sum(slot_weight[:, :, None] * slot_answer.astype(jnp.float32), axis=1)]
  transfers between devices with their start and end apart: 4 -> 6, of which waited for: 4 -> 1; matrix products, arithmetic and copies ran while one was open for 43% -> 3% of each run, Pallas kernels for 0% -> 29%
where the time goes in v1:
time: 39.5 us; the launch traced here: 39.1 us
  Pallas kernels  13.5 us (34%)
  local copies, waits for them, and re-layouts  11.6 us (29%)
  starting transfers between devices  8.11 us (21%)
  waiting for transfers between devices  5.83 us (15%)
    pallas_call x6, Pallas kernels, call(): pl.pallas_call(kernel, out_shape=jax.ShapeDtypeStruct(shape, dtype), in_s...  13.5 us
    unnamed x26, local copies, waits for them, and re-layouts  11.6 us
    ppermute x6, starting transfers between devices, send(): lax.ppermute(array, 'expert', [(i, path(i)) for i in range(devices_n)])  8.11 us
    ppermute x6, waiting for transfers between devices, send(): lax.ppermute(array, 'expert', [(i, path(i)) for i in range(devices_n)])  5.83 us
  transfers between devices with their start and end apart: 6, of which 1 were waited for; matrix products, arithmetic and copies ran while one was open for 3% of the time, Pallas kernels for 29%

profile of v1, /device:TPU:0, one launch (start us, length us, event | category | flops | bytes accessed | tf_op | source)
XLA Modules:
  0.0 39.1 jit_solution(16393238227341989476)
XLA Ops:
  0.0 2.9 %collective-permute-start = (bf16[64,2048]{1,0:T(8,128)(2,1)}, bf16[64,2048]{1,0:T(8,128)(2,1)S(1)}, u32[]{:S(2)}, u32[]{:S(2)}) collective-permute-start(bf16[64,2048]{1,0:T(8,128)(2,1)} %inputs_ref.1), channel_id=1, source_target_pairs={{0,1},{1,0},{2,3},{3,2},{4,5},{5,4},{6,7},{7,6},{8,9},{9,8},{10,11... | collective-permute-start | bytes 786440 | tf_op jit(solution)/shard_map/ppermute | solution.py:101
  2.9 1.5 %collective-permute-start.2 = (bf16[64,2048]{1,0:T(8,128)(2,1)}, bf16[64,2048]{1,0:T(8,128)(2,1)S(1)}, u32[]{:S(2)}, u32[]{:S(2)}) collective-permute-start(bf16[64,2048]{1,0:T(8,128)(2,1)} %inputs_ref.1), channel_id=1, source_target_pairs={{0,2},{1,3},{2,0},{3,1},{4,6},{5,7},{6,4},{7,5},{8,10},{9,11},{10,... | collective-permute-start | bytes 786440 | tf_op jit(solution)/shard_map/ppermute | solution.py:101
  4.5 0.0 collective-permute-start.4
  4.5 5.8 %collective-permute-done.inputs_ref = bf16[64,2048]{1,0:T(8,128)(2,1)S(1)} collective-permute-done((bf16[64,2048]{1,0:T(8,128)(2,1)}, bf16[64,2048]{1,0:T(8,128)(2,1)S(1)}, u32[]{:S(2)}, u32[]{:S(2)}) %collective-permute-start) | collective-permute-done | bytes 262176 | tf_op jit(solution)/shard_map/ppermute | solution.py:101
  10.3 1.9 %copy-done = bf16[1,2048,768]{2,1,0:T(8,128)(2,1)S(1)} copy-done((bf16[1,2048,768]{2,1,0:T(8,128)(2,1)S(1)}, bf16[1,2048,768]{2,1,0:T(8,128)(2,1)}, u32[]{:S(2)}) %copy-start) | copy-done | bytes 3145752
  12.2 1.9 %copy-done.2 = bf16[1,2048,768]{2,1,0:T(8,128)(2,1)S(1)} copy-done((bf16[1,2048,768]{2,1,0:T(8,128)(2,1)S(1)}, bf16[1,2048,768]{2,1,0:T(8,128)(2,1)}, u32[]{:S(2)}) %copy-start.2) | copy-done | bytes 3145752
  14.1 1.9 %copy-done.4 = bf16[1,768,2048]{2,1,0:T(8,128)(2,1)S(1)} copy-done((bf16[1,768,2048]{2,1,0:T(8,128)(2,1)S(1)}, bf16[1,768,2048]{2,1,0:T(8,128)(2,1)}, u32[]{:S(2)}) %copy-start.4) | copy-done | bytes 3145752
  16.0 2.5 %shard_map.84 = bf16[64,2048]{1,0:T(8,128)(2,1)} custom-call(bf16[64,2048]{1,0:T(8,128)(2,1)S(1)} %collective-permute-done.inputs_ref, bf16[1,2048,768]{2,1,0:T(8,128)(2,1)S(1)} %copy-done, bf16[1,2048,768]{2,1,0:T(8,128)(2,1)S(1)} %copy-done.2, bf16[1,768,2048]{2,1,0:T(8,128)(2,1)S(1)} %copy-done.4), custom_call_target="tpu_custom_call" | custom-call | flops 603979776 | bytes 9437184 | tf_op jit(solution)/shard_map/pallas_call | solution.py:76
  18.4 2.1 %collective-permute-start.1 = (bf16[64,2048]{1,0:T(8,128)(2,1)}, bf16[64,2048]{1,0:T(8,128)(2,1)}, u32[]{:S(2)}, u32[]{:S(2)}) collective-permute-start(bf16[64,2048]{1,0:T(8,128)(2,1)} %shard_map.84), channel_id=1, source_target_pairs={{0,1},{1,0},{2,3},{3,2},{4,5},{5,4},{6,7},{7,6},{8,9},{9,8},{10,11... | collective-permute-start | bytes 786440 | tf_op jit(solution)/shard_map/ppermute | solution.py:101
  20.5 0.0 collective-permute-done.2.inputs_ref
  20.5 2.5 %shard_map.85 = bf16[64,2048]{1,0:T(8,128)(2,1)} custom-call(bf16[64,2048]{1,0:T(8,128)(2,1)S(1)} %collective-permute-done.2.inputs_ref, bf16[1,2048,768]{2,1,0:T(8,128)(2,1)S(1)} %copy-done, bf16[1,2048,768]{2,1,0:T(8,128)(2,1)S(1)} %copy-done.2, bf16[1,768,2048]{2,1,0:T(8,128)(2,1)S(1)} %copy-done.4), custom_call_target="tpu_custom_call" | custom-call | flops 603979776 | bytes 9437184 | tf_op jit(solution)/shard_map/pallas_call | solution.py:76
  23.0 0.0 copy-start.9
  23.0 1.6 %collective-permute-start.3 = (bf16[64,2048]{1,0:T(8,128)(2,1)}, bf16[64,2048]{1,0:T(8,128)(2,1)}, u32[]{:S(2)}, u32[]{:S(2)}) collective-permute-start(bf16[64,2048]{1,0:T(8,128)(2,1)} %shard_map.85), channel_id=1, source_target_pairs={{0,2},{1,3},{2,0},{3,1},{4,6},{5,7},{6,4},{7,5},{8,10},{9,11},{10,... | collective-permute-start | bytes 786440 | tf_op jit(solution)/shard_map/ppermute | solution.py:101
  24.6 0.0 collective-permute-done.4.inputs_ref
  24.6 2.5 %shard_map.86 = bf16[64,2048]{1,0:T(8,128)(2,1)} custom-call(bf16[64,2048]{1,0:T(8,128)(2,1)S(1)} %collective-permute-done.4.inputs_ref, bf16[1,2048,768]{2,1,0:T(8,128)(2,1)S(1)} %copy-done, bf16[1,2048,768]{2,1,0:T(8,128)(2,1)S(1)} %copy-done.2, bf16[1,768,2048]{2,1,0:T(8,128)(2,1)S(1)} %copy-done.4), custom_call_target="tpu_custom_call" | custom-call | flops 603979776 | bytes 9437184 | tf_op jit(solution)/shard_map/pallas_call | solution.py:76
  27.1 0.0 collective-permute-start.5
  27.1 0.0 copy-done.10
  27.1 1.1 %copy.9.router_ref = bf16[2048,4]{1,0:T(8,128)(2,1)} copy(bf16[2048,4]{0,1:T(4,128)(2,1)S(1)} %copy-done.10) | data formatting | bytes 32768 | tf_op args[1]
  28.2 0.0 copy-done.11
  28.2 0.1 copy.10.routing_ref
  28.3 0.0 copy-done.7
  28.3 1.0 %copy-done.6 = bf16[2048,4]{1,0:T(8,128)(2,1)S(1)} copy-done((bf16[2048,4]{1,0:T(8,128)(2,1)S(1)}, bf16[2048,4]{1,0:T(8,128)(2,1)}, u32[]{:S(2)}) %copy-start.6) | copy-done | bytes 16408
  29.3 2.1 %shard_map.82.share_ref = f32[64,128]{1,0:T(8,128)S(1)} custom-call(s32[1]{0:T(128)} %bitcast.me_ref, s32[2]{0:T(128)S(1)} %copy-done.9, bf16[64,2048]{1,0:T(8,128)(2,1)S(1)} %copy-done.7, bf16[2048,4]{1,0:T(8,128)(2,1)S(1)} %copy-done.6, s32[64,4]{1,0:T(8,128)S(1)} %copy.10.routing_ref, s32[1,256]{1,0:T(1,128)S(1)} %copy-done.8), custom_call_target="tpu_custom_call" | custom-call | tf_op jit(solution)/shard_map/pallas_call | solution.py:76
  31.4 0.0 copy-done.1
  31.5 0.0 copy-start.3
  31.5 1.9 %copy-done.3 = bf16[1,2048,768]{2,1,0:T(8,128)(2,1)S(1)} copy-done((bf16[1,2048,768]{2,1,0:T(8,128)(2,1)S(1)}, bf16[1,2048,768]{2,1,0:T(8,128)(2,1)}, u32[]{:S(2)}) %copy-start.3) | copy-done | bytes 3145752
  33.3 1.9 %copy-done.5 = bf16[1,768,2048]{2,1,0:T(8,128)(2,1)S(1)} copy-done((bf16[1,768,2048]{2,1,0:T(8,128)(2,1)S(1)}, bf16[1,768,2048]{2,1,0:T(8,128)(2,1)}, u32[]{:S(2)}) %copy-start.5) | copy-done | bytes 3145752
  35.2 1.8 %shard_map.83.refs_0_ = bf16[64,2048]{1,0:T(8,128)(2,1)S(1)} custom-call(bf16[64,2048]{1,0:T(8,128)(2,1)S(1)} %copy-done.7, bf16[1,2048,768]{2,1,0:T(8,128)(2,1)S(1)} %copy-done.1, bf16[1,2048,768]{2,1,0:T(8,128)(2,1)S(1)} %copy-done.3, bf16[1,768,2048]{2,1,0:T(8,128)(2,1)S(1)} %copy-done.5), custom_call_target="tpu_custom_call" | custom-call | flops 603979776 | bytes 9437184 | tf_op jit(solution)/shard_map/pallas_call | solution.py:76
  37.0 0.0 collective-permute-done.1.refs_1_
  37.0 0.0 collective-permute-done.3.refs_2_
  37.0 0.0 collective-permute-done.5.refs_3_
  37.1 2.1 %shard_map.87 = bf16[64,2048]{1,0:T(8,128)(2,1)} custom-call(f32[64,128]{1,0:T(8,128)S(1)} %shard_map.82.share_ref, bf16[64,2048]{1,0:T(8,128)(2,1)S(1)} %shard_map.83.refs_0_, bf16[64,2048]{1,0:T(8,128)(2,1)} %collective-permute-done.1.refs_1_, bf16[64,2048]{1,0:T(8,128)(2,1)} %collective-permute-done.3.refs_2_, bf16[64,2048]{1,0:T(8,128)(2,1)} %collective-permute-done.5.refs_3_), custom_call_target="tpu_custom_call" | custom-call | tf_op jit(solution)/shard_map/pallas_call | solution.py:76
  (12 shorter events, 0.0 us)
Async XLA Ops:
  0.0 10.3 %collective-permute-start = (bf16[64,2048]{1,0:T(8,128)(2,1)}, bf16[64,2048]{1,0:T(8,128)(2,1)S(1)}, u32[]{:S(2)}, u32[]{:S(2)}) collective-permute-start(bf16[64,2048]{1,0:T(8,128)(2,1)} %inputs_ref.1), channel_id=1, source_target_pairs={{0,1},{1,0},{2,3},{3,2},{4,5},{5,4},{6,7},{7,6},{8,9},{9,8},{10,11... | collective-permute-start | bytes 786440 | tf_op jit(solution)/shard_map/ppermute | solution.py:101
  2.9 17.6 %collective-permute-start.2 = (bf16[64,2048]{1,0:T(8,128)(2,1)}, bf16[64,2048]{1,0:T(8,128)(2,1)S(1)}, u32[]{:S(2)}, u32[]{:S(2)}) collective-permute-start(bf16[64,2048]{1,0:T(8,128)(2,1)} %inputs_ref.1), channel_id=1, source_target_pairs={{0,2},{1,3},{2,0},{3,1},{4,6},{5,7},{6,4},{7,5},{8,10},{9,11},{10,... | collective-permute-start | bytes 786440 | tf_op jit(solution)/shard_map/ppermute | solution.py:101
  4.5 20.2 %collective-permute-start.4 = (bf16[64,2048]{1,0:T(8,128)(2,1)}, bf16[64,2048]{1,0:T(8,128)(2,1)S(1)}, u32[]{:S(2)}, u32[]{:S(2)}) collective-permute-start(bf16[64,2048]{1,0:T(8,128)(2,1)} %inputs_ref.1), channel_id=1, source_target_pairs={{0,3},{1,2},{2,1},{3,0},{4,7},{5,6},{6,5},{7,4},{8,11},{9,10},{10,... | collective-permute-start | bytes 786440 | tf_op jit(solution)/shard_map/ppermute | solution.py:101
  10.3 1.9 %copy-start = (bf16[1,2048,768]{2,1,0:T(8,128)(2,1)S(1)}, bf16[1,2048,768]{2,1,0:T(8,128)(2,1)}, u32[]{:S(2)}) copy-start(bf16[1,2048,768]{2,1,0:T(8,128)(2,1)} %gate_ref.7) | copy-start | bytes 9437188
  12.2 1.9 %copy-start.2 = (bf16[1,2048,768]{2,1,0:T(8,128)(2,1)S(1)}, bf16[1,2048,768]{2,1,0:T(8,128)(2,1)}, u32[]{:S(2)}) copy-start(bf16[1,2048,768]{2,1,0:T(8,128)(2,1)} %up_ref.7) | copy-start | bytes 9437188
  14.1 1.9 %copy-start.4 = (bf16[1,768,2048]{2,1,0:T(8,128)(2,1)S(1)}, bf16[1,768,2048]{2,1,0:T(8,128)(2,1)}, u32[]{:S(2)}) copy-start(bf16[1,768,2048]{2,1,0:T(8,128)(2,1)} %down_ref.7) | copy-start | bytes 9437188
  18.4 18.6 %collective-permute-start.1 = (bf16[64,2048]{1,0:T(8,128)(2,1)}, bf16[64,2048]{1,0:T(8,128)(2,1)}, u32[]{:S(2)}, u32[]{:S(2)}) collective-permute-start(bf16[64,2048]{1,0:T(8,128)(2,1)} %shard_map.84), channel_id=1, source_target_pairs={{0,1},{1,0},{2,3},{3,2},{4,5},{5,4},{6,7},{7,6},{8,9},{9,8},{10,11... | collective-permute-start | bytes 786440 | tf_op jit(solution)/shard_map/ppermute | solution.py:101
  23.0 4.1 %copy-start.10 = (bf16[2048,4]{0,1:T(4,128)(2,1)S(1)}, bf16[2048,4]{0,1:T(4,128)(2,1)}, u32[]{:S(2)}) copy-start(bf16[2048,4]{0,1:T(4,128)(2,1)} %param.9) | copy-start | bytes 49156
  23.0 5.2 %copy-start.11 = (s32[64,4]{0,1:T(4,128)S(1)}, s32[64,4]{0,1:T(4,128)}, u32[]{:S(2)}) copy-start(s32[64,4]{0,1:T(4,128)} %param.13) | copy-start | bytes 3076
  23.0 5.3 %copy-start.7 = (bf16[64,2048]{1,0:T(8,128)(2,1)S(1)}, bf16[64,2048]{1,0:T(8,128)(2,1)}, u32[]{:S(2)}) copy-start(bf16[64,2048]{1,0:T(8,128)(2,1)} %inputs_ref.1) | copy-start | bytes 786436
  23.0 5.3 %copy-start.8 = (s32[1,256]{1,0:T(1,128)S(1)}, s32[1,256]{1,0:T(1,128)}, u32[]{:S(2)}) copy-start(s32[1,256]{1,0:T(1,128)} %priority_ref.1) | copy-start | bytes 3076
  23.0 5.3 %copy-start.9 = (s32[2]{0:T(128)S(1)}, s32[2]{0:T(128)}, u32[]{:S(2)}) copy-start(s32[2]{0:T(128)} %hot_ref.1) | copy-start | bytes 28
  23.0 14.0 %collective-permute-start.3 = (bf16[64,2048]{1,0:T(8,128)(2,1)}, bf16[64,2048]{1,0:T(8,128)(2,1)}, u32[]{:S(2)}, u32[]{:S(2)}) collective-permute-start(bf16[64,2048]{1,0:T(8,128)(2,1)} %shard_map.85), channel_id=1, source_target_pairs={{0,2},{1,3},{2,0},{3,1},{4,6},{5,7},{6,4},{7,5},{8,10},{9,11},{10,... | collective-permute-start | bytes 786440 | tf_op jit(solution)/shard_map/ppermute | solution.py:101
  24.6 6.8 %copy-start.1 = (bf16[1,2048,768]{2,1,0:T(8,128)(2,1)S(1)}, bf16[1,2048,768]{2,1,0:T(8,128)(2,1)}, u32[]{:S(2)}) copy-start(bf16[1,2048,768]{2,1,0:T(8,128)(2,1)} %gate_ref.7) | copy-start | bytes 9437188
  27.1 9.9 %collective-permute-start.5 = (bf16[64,2048]{1,0:T(8,128)(2,1)}, bf16[64,2048]{1,0:T(8,128)(2,1)}, u32[]{:S(2)}, u32[]{:S(2)}) collective-permute-start(bf16[64,2048]{1,0:T(8,128)(2,1)} %shard_map.86), channel_id=1, source_target_pairs={{0,3},{1,2},{2,1},{3,0},{4,7},{5,6},{6,5},{7,4},{8,11},{9,10},{10,... | collective-permute-start | bytes 786440 | tf_op jit(solution)/shard_map/ppermute | solution.py:101
  28.3 1.0 %copy-start.6 = (bf16[2048,4]{1,0:T(8,128)(2,1)S(1)}, bf16[2048,4]{1,0:T(8,128)(2,1)}, u32[]{:S(2)}) copy-start(bf16[2048,4]{1,0:T(8,128)(2,1)} %copy.9.router_ref) | copy-start | bytes 49156
  31.5 1.9 %copy-start.3 = (bf16[1,2048,768]{2,1,0:T(8,128)(2,1)S(1)}, bf16[1,2048,768]{2,1,0:T(8,128)(2,1)}, u32[]{:S(2)}) copy-start(bf16[1,2048,768]{2,1,0:T(8,128)(2,1)} %up_ref.7) | copy-start | bytes 9437188
  33.3 1.9 %copy-start.5 = (bf16[1,768,2048]{2,1,0:T(8,128)(2,1)S(1)}, bf16[1,768,2048]{2,1,0:T(8,128)(2,1)}, u32[]{:S(2)}) copy-start(bf16[1,768,2048]{2,1,0:T(8,128)(2,1)} %down_ref.7) | copy-start | bytes 9437188

commit v2 on v1

v2 whole, which is shorter than its diff:
```python
import functools

import jax
import jax.numpy as jnp
from jax import lax
from jax.experimental import pallas as pl
from jax.experimental.pallas import tpu as pltpu
from jax.sharding import PartitionSpec as P

VMEM = pl.BlockSpec(memory_space=pltpu.VMEM)
SMEM = pl.BlockSpec(memory_space=pltpu.SMEM)
HBM = pl.BlockSpec(memory_space=pltpu.HBM)
ROOM = 24 << 20
FIRST_ROOM = 43 << 20
ANY = pl.BlockSpec(memory_space=pl.ANY)
LANES = 128


def kept_shares(capacity, peers, me, hot, tokens, router, routing, priority):
    logits = lax.dot_general(tokens, router, (((1,), (1,)), ((), ())), preferred_element_type=jnp.float32)
    sigmas = 1.0 / (1.0 + jnp.exp(-logits))
    top, rows = routing.shape
    slots = rows * top
    expert_at = lax.broadcasted_iota(jnp.int32, sigmas.shape, 1)
    choice = lax.broadcasted_iota(jnp.int32, (rows, slots), 1) - top * lax.broadcasted_iota(
        jnp.int32, (rows, slots), 0
    )
    square = lax.broadcasted_iota(jnp.int32, (rows, rows), 0) == lax.broadcasted_iota(jnp.int32, (rows, rows), 1)
    priority = jnp.broadcast_to(priority, (rows, slots))
    columns = [
        jnp.sum(jnp.where(square, routing[k : k + 1, :], 0), axis=1, keepdims=True) for k in range(top)
    ]
    slot_priority = [
        jnp.sum(jnp.where(choice == k, priority, 0), axis=1, keepdims=True) for k in range(top)
    ]
    slot_expert = jnp.zeros((1, slots), jnp.int32)
    total = jnp.zeros((rows, 1), jnp.float32)
    for k in range(top):
        slot_expert += jnp.sum(jnp.where(choice == k, columns[k], 0), axis=0, keepdims=True)
        total += jnp.sum(jnp.where(expert_at == columns[k], sigmas, 0.0), axis=1, keepdims=True)
    lane = lax.broadcasted_iota(jnp.int32, (rows, LANES), 1)
    share = jnp.zeros((rows, LANES), jnp.float32)
    for d, peer in enumerate(peers):
        expert = peer(me)
        here = jnp.zeros((rows, 1), jnp.int32)
        mine = jnp.zeros((rows, 1), jnp.int32)
        for k in range(top):
            at = columns[k] == expert
            here += at.astype(jnp.int32)
            mine += jnp.where(at, slot_priority[k], 0)
        rank = jnp.sum(
            ((slot_expert == expert) & (priority < mine)).astype(jnp.int32), axis=1, keepdims=True
        )
        is_hot = jnp.int32(0)
        for h in hot:
            is_hot += (h == expert).astype(jnp.int32)
        keeping = (here > 0) & ((rank < capacity) | (is_hot > 0))
        sigma = jnp.sum(jnp.where(expert_at == expert, sigmas, 0.0), axis=1, keepdims=True)
        share = jnp.where(lane == d, jnp.where(keeping, sigma / total, 0.0), share)
    return share


def swiglu(inputs, gate, up, down):
    gate_part = jnp.dot(inputs, gate(), preferred_element_type=jnp.float32)
    up_part = jnp.dot(inputs, up(), preferred_element_type=jnp.float32)
    hidden = (gate_part / (1.0 + jnp.exp(-gate_part)) * up_part).astype(jnp.bfloat16)
    return jnp.dot(hidden, down(), preferred_element_type=jnp.float32)


def share_kernel(capacity, peers, me_ref, hot_ref, tokens_ref, router_ref, routing_ref, priority_ref, *refs):
    hot = [hot_ref[h] for h in range(hot_ref.shape[0])]
    refs[-1][...] = kept_shares(
        capacity, peers, me_ref[0], hot, tokens_ref[...], router_ref[...], routing_ref[...], priority_ref[...]
    )


def first_kernel(tokens_ref, gate_in, up_in, down_in, own_ref, gate_ref, up_ref, down_ref, sems):
    pairs = [(gate_in, gate_ref), (up_in, up_ref), (down_in, down_ref)]
    copies = [pltpu.make_async_copy(src, dst, sems.at[i]) for i, (src, dst) in enumerate(pairs)]
    for copy in copies:
        copy.start()

    def landed(copy, ref):
        def get():
            copy.wait()
            return ref[0]

        return get

    weights = [landed(copy, ref) for copy, (_, ref) in zip(copies, pairs)]
    own_ref[...] = swiglu(tokens_ref[...], *weights).astype(own_ref.dtype)


def expert_kernel(count, *refs):
    inputs, (gate_ref, up_ref, down_ref), answers = refs[:count], refs[count : count + 3], refs[-count:]
    rows = [ref[...] for ref in inputs]
    result = swiglu(
        rows[0] if count == 1 else jnp.concatenate(rows), lambda: gate_ref[0], lambda: up_ref[0], lambda: down_ref[0]
    ).astype(answers[0].dtype)
    step = rows[0].shape[0]
    for i, ref in enumerate(answers):
        ref[...] = result[i * step : (i + 1) * step]


def mix_kernel(share_ref, *refs):
    *answers, mixed_ref = refs
    total = share_ref[:, 0:1] * answers[0][...].astype(jnp.float32)
    for d in range(1, len(answers)):
        total += share_ref[:, d : d + 1] * answers[d][...].astype(jnp.float32)
    mixed_ref[...] = total.astype(mixed_ref.dtype)


def call(kernel, outs, operands, specs=None, scratch=(), cost=None, room=ROOM):
    return pl.pallas_call(
        kernel,
        out_shape=outs,
        in_specs=specs or [VMEM] * len(operands),
        out_specs=jax.tree.map(lambda _: VMEM, outs),
        scratch_shapes=scratch,
        compiler_params=pltpu.CompilerParams(vmem_limit_bytes=room),
        cost_estimate=cost,
    )(*operands)


def groups(devices_n):
    order = list(range(devices_n - 1, 0, -1))
    return [order[:1]] + [order[i : i + 2] for i in range(1, len(order), 2)]


def shards(tokens, router_weight, gate_weight, up_weight, down_weight, routing, priority, hot_list):
    devices_n = lax.axis_size("expert")
    tok_count, width = tokens.shape
    top_count = routing.shape[1]
    hidden_n = gate_weight.shape[2]
    slot_count = tok_count * top_count
    capacity = min(tok_count, 3 * slot_count // (2 * devices_n))
    me = lax.axis_index("expert").astype(jnp.int32).reshape(1)
    if devices_n & (devices_n - 1) == 0:
        paths = [(lambda i, d=d: i ^ d) for d in range(devices_n)]
        backs = paths
    else:
        paths = [(lambda i, d=d: (i + d) % devices_n) for d in range(devices_n)]
        backs = [(lambda i, d=d: (i + devices_n - d) % devices_n) for d in range(devices_n)]

    def send(array, path):
        return lax.ppermute(array, "expert", [(i, path(i)) for i in range(devices_n)])

    def like(array):
        return jax.ShapeDtypeStruct(array.shape, array.dtype)

    def cost(rows):
        return pl.CostEstimate(
            flops=6 * rows * width * hidden_n, bytes_accessed=6 * width * hidden_n, transcendentals=0
        )

    def experts(blocks, weights, after=()):
        count = len(blocks)
        return call(
            functools.partial(expert_kernel, count),
            (like(tokens),) * count,
            (*blocks, *weights, *after),
            [VMEM] * (count + 3) + [ANY] * len(after),
            cost=cost(tok_count * count),
        )

    order = range(devices_n - 1, 0, -1)
    arrived = {d: send(tokens, paths[d]) for d in order}
    own, *weights = call(
        first_kernel,
        (like(tokens), like(gate_weight), like(up_weight), like(down_weight)),
        (tokens, gate_weight, up_weight, down_weight),
        [VMEM, HBM, HBM, HBM],
        [pltpu.SemaphoreType.DMA((3,))],
        cost(tok_count),
        FIRST_ROOM,
    )
    answers = {0: own}
    last = ()
    for group in groups(devices_n):
        results = experts([arrived[d] for d in group], weights)
        last = results[:1]
        for d, result in zip(group, results):
            answers[d] = send(result, backs[d])
    share = call(
        functools.partial(share_kernel, capacity, paths),
        jax.ShapeDtypeStruct((tok_count, LANES), jnp.float32),
        (me, hot_list, tokens, router_weight.T, routing.T, priority, *last),
        [SMEM, SMEM] + [VMEM] * 4 + [ANY] * len(last),
    )
    return call(mix_kernel, like(tokens), (share, *[answers[d] for d in range(devices_n)]))


def solution(mesh):
    return jax.shard_map(
        shards,
        mesh=mesh,
        in_specs=(
            P(("dp", "expert"), None),
            P(),
            P("expert", None, None),
            P("expert", None, None),
            P("expert", None, None),
            P(("dp", "expert"), None),
            P(("dp", "expert"), None),
            P("dp"),
        ),
        out_specs=P(("dp", "expert"), None),
        check_vma=False,
    )
```

time: 39.5 us -> 28.6 us (0.72)
  local copies, waits for them, and re-layouts: 11.6 us -> 1.04 us
  Pallas kernels: 13.5 us -> 9.69 us
  waiting for transfers between devices: 5.83 us -> 8.07 us
  starting transfers between devices: 8.11 us -> 9.64 us
    unnamed x26 -> x12, local copies, waits for them, and re-layouts: 11.6 us -> 1.04 us
    pallas_call x6 -> x5, Pallas kernels: 13.5 us -> 9.69 us  [call(): pl.pallas_call(kernel, out_shape=outs, in_specs=specs or [VMEM] * len(ope...]
    ppermute x6, waiting for transfers between devices: 5.83 us -> 8.07 us  [send(): lax.ppermute(array, 'expert', [(i, path(i)) for i in range(devices_n)])]
    ppermute x6, starting transfers between devices: 8.11 us -> 9.64 us  [send(): lax.ppermute(array, 'expert', [(i, path(i)) for i in range(devices_n)])]
  transfers between devices with their start and end apart: 6 -> 6, of which waited for: 1 -> 4; matrix products, arithmetic and copies ran while one was open for 3% -> 0% of each run, Pallas kernels for 29% -> 31%
where the time goes in v2:
time: 28.6 us; the launch traced here: 28.5 us
  Pallas kernels  9.69 us (34%)
  starting transfers between devices  9.64 us (34%)
  waiting for transfers between devices  8.07 us (28%)
  local copies, waits for them, and re-layouts  1.04 us (4%)
    pallas_call x5, Pallas kernels, call(): pl.pallas_call(kernel, out_shape=outs, in_specs=specs or [VMEM] * len(ope...  9.69 us
    ppermute x6, starting transfers between devices, send(): lax.ppermute(array, 'expert', [(i, path(i)) for i in range(devices_n)])  9.64 us
    ppermute x6, waiting for transfers between devices, send(): lax.ppermute(array, 'expert', [(i, path(i)) for i in range(devices_n)])  8.07 us
    unnamed x12, local copies, waits for them, and re-layouts  1.04 us
  transfers between devices with their start and end apart: 6, of which 4 were waited for; matrix products, arithmetic and copies ran while one was open for 0% of the time, Pallas kernels for 31%

profile of v2, /device:TPU:0, one launch (start us, length us, event | category | flops | bytes accessed | tf_op | source)
XLA Modules:
  0.0 28.5 jit_solution(9693516267334878707)
XLA Ops:
  0.0 3.0 %collective-permute-start = (bf16[64,2048]{1,0:T(8,128)(2,1)}, bf16[64,2048]{1,0:T(8,128)(2,1)S(1)}, u32[]{:S(2)}, u32[]{:S(2)}) collective-permute-start(bf16[64,2048]{1,0:T(8,128)(2,1)} %tokens_ref.3), channel_id=1, source_target_pairs={{0,2},{1,3},{2,0},{3,1},{4,6},{5,7},{6,4},{7,5},{8,10},{9,11},{10,... | collective-permute-start | bytes 786440 | tf_op jit(solution)/shard_map/ppermute | solution.py:146
  3.0 1.5 %collective-permute-start.1 = (bf16[64,2048]{1,0:T(8,128)(2,1)}, bf16[64,2048]{1,0:T(8,128)(2,1)S(1)}, u32[]{:S(2)}, u32[]{:S(2)}) collective-permute-start(bf16[64,2048]{1,0:T(8,128)(2,1)} %tokens_ref.3), channel_id=1, source_target_pairs={{0,1},{1,0},{2,3},{3,2},{4,5},{5,4},{6,7},{7,6},{8,9},{9,8},{10,11... | collective-permute-start | bytes 786440 | tf_op jit(solution)/shard_map/ppermute | solution.py:146
  4.5 0.0 collective-permute-start.4
  4.5 0.0 copy-start
  4.5 1.0 %copy-done = bf16[64,2048]{1,0:T(8,128)(2,1)S(1)} copy-done((bf16[64,2048]{1,0:T(8,128)(2,1)S(1)}, bf16[64,2048]{1,0:T(8,128)(2,1)}, u32[]{:S(2)}) %copy-start) | copy-done | bytes 262168
  5.5 4.4 %shard_map.82 = (bf16[64,2048]{1,0:T(8,128)(2,1)S(1)}, bf16[1,2048,768]{2,1,0:T(8,128)(2,1)S(1)}, bf16[1,2048,768]{2,1,0:T(8,128)(2,1)S(1)}, bf16[1,768,2048]{2,1,0:T(8,128)(2,1)S(1)}) custom-call(bf16[64,2048]{1,0:T(8,128)(2,1)S(1)} %copy-done, bf16[1,2048,768]{2,1,0:T(8,128)(2,1)} %gate_in.1, bf16[1,2048,768]{2,1,0:T(8,128)(2,1)} %up_in.1, ...), custom_call_target="tpu_custom_call" | custom-call | flops 603979776 | bytes 9437184 | tf_op jit(solution)/shard_map/pallas_call | solution.py:114
  9.9 0.0 collective-permute-done.refs_0_
  9.9 2.5 %collective-permute-done.1.refs_1_ = bf16[64,2048]{1,0:T(8,128)(2,1)S(1)} collective-permute-done((bf16[64,2048]{1,0:T(8,128)(2,1)}, bf16[64,2048]{1,0:T(8,128)(2,1)S(1)}, u32[]{:S(2)}, u32[]{:S(2)}) %collective-permute-start.1) | collective-permute-done | bytes 262176 | tf_op jit(solution)/shard_map/ppermute | solution.py:146
  12.4 1.5 %shard_map.83 = (bf16[64,2048]{1,0:T(8,128)(2,1)S(1)}, bf16[64,2048]{1,0:T(8,128)(2,1)S(1)}) custom-call(bf16[64,2048]{1,0:T(8,128)(2,1)S(1)} %collective-permute-done.refs_0_, bf16[64,2048]{1,0:T(8,128)(2,1)S(1)} %collective-permute-done.1.refs_1_, bf16[1,2048,768]{2,1,0:T(8,128)(2,1)S(1)} %get-tuple-element.11.refs_2_.refs_1_, ...), custom_call_target="tpu_custom_call" | custom-call | flops 1207959552 | bytes 9437184 | tf_op jit(solution)/shard_map/pallas_call | solution.py:114
  13.9 1.6 %collective-permute-start.2 = (bf16[64,2048]{1,0:T(8,128)(2,1)S(1)}, bf16[64,2048]{1,0:T(8,128)(2,1)S(1)}, u32[]{:S(2)}, u32[]{:S(2)}) collective-permute-start(bf16[64,2048]{1,0:T(8,128)(2,1)S(1)} %get-tuple-element.16), channel_id=1, source_target_pairs={{0,1},{1,0},{2,3},{3,2},{4,5},{5,4},{6,7},{7,6},{8,9},{9,8},{10,11... | collective-permute-start | bytes 786440 | tf_op jit(solution)/shard_map/ppermute | solution.py:146
  15.5 0.0 copy-start.1
  15.5 0.0 copy-start.2
  15.5 0.0 copy-start.3
  15.5 0.0 copy-start.4
  15.5 0.0 copy-start.5
  15.5 0.6 %collective-permute-start.3 = (bf16[64,2048]{1,0:T(8,128)(2,1)S(1)}, bf16[64,2048]{1,0:T(8,128)(2,1)S(1)}, u32[]{:S(2)}, u32[]{:S(2)}) collective-permute-start(bf16[64,2048]{1,0:T(8,128)(2,1)S(1)} %get-tuple-element.14.refs_0_), channel_id=1, source_target_pairs={{0,2},{1,3},{2,0},{3,1},{4,6},{5,7},{6,4},{7,5},{8,10},{9,11},{10,... | collective-permute-start | bytes 786440 | tf_op jit(solution)/shard_map/ppermute | solution.py:146
  16.0 1.4 %collective-permute-done.4.refs_0_ = bf16[64,2048]{1,0:T(8,128)(2,1)S(1)} collective-permute-done((bf16[64,2048]{1,0:T(8,128)(2,1)}, bf16[64,2048]{1,0:T(8,128)(2,1)S(1)}, u32[]{:S(2)}, u32[]{:S(2)}) %collective-permute-start.4) | collective-permute-done | bytes 262176 | tf_op jit(solution)/shard_map/ppermute | solution.py:146
  17.4 1.8 %shard_map.85 = bf16[64,2048]{1,0:T(8,128)(2,1)S(1)} custom-call(bf16[64,2048]{1,0:T(8,128)(2,1)S(1)} %collective-permute-done.4.refs_0_, bf16[1,2048,768]{2,1,0:T(8,128)(2,1)S(1)} %get-tuple-element.11.refs_2_.refs_1_, bf16[1,2048,768]{2,1,0:T(8,128)(2,1)S(1)} %get-tuple-element.12.refs_3_.refs_2_, bf16[1,768,2048]{2,1,0:T(8,128)(2,1)S(1)} %get-tuple-element.13.refs_4_.refs_3_), custom_call_target="tpu_custom_call" | custom-call | flops 603979776 | bytes 9437184 | tf_op jit(solution)/shard_map/pallas_call | solution.py:114
  19.2 3.0 %collective-permute-start.5 = (bf16[64,2048]{1,0:T(8,128)(2,1)S(1)}, bf16[64,2048]{1,0:T(8,128)(2,1)S(1)}, u32[]{:S(2)}, u32[]{:S(2)}) collective-permute-start(bf16[64,2048]{1,0:T(8,128)(2,1)S(1)} %shard_map.85), channel_id=1, source_target_pairs={{0,3},{1,2},{2,1},{3,0},{4,7},{5,6},{6,5},{7,4},{8,11},{9,10},{10,... | collective-permute-start | bytes 786440 | tf_op jit(solution)/shard_map/ppermute | solution.py:146
  22.3 0.0 copy-done.1
  22.3 0.0 copy-done.2
  22.3 0.0 copy-done.3
  22.3 0.0 copy-done.4
  22.3 0.0 copy-done.5
  22.3 1.0 %shard_map.84.share_ref = f32[64,128]{1,0:T(8,128)S(1)} custom-call(s32[1]{0:T(128)} %bitcast.me_ref, s32[2]{0:T(128)S(1)} %copy-done.5, bf16[64,2048]{1,0:T(8,128)(2,1)S(1)} %copy-done.1, bf16[4,2048]{1,0:T(4,128)(2,1)S(1)} %bitcast.3, s32[4,64]{1,0:T(4,128)S(1)} %bitcast.4, s32[1,256]{1,0:T(1,128)S(1)} %copy-done.4, ...), custom_call_target="tpu_custom_call" | custom-call | tf_op jit(solution)/shard_map/pallas_call | solution.py:114
  23.3 0.3 %collective-permute-done.2.refs_1_ = bf16[64,2048]{1,0:T(8,128)(2,1)S(1)} collective-permute-done((bf16[64,2048]{1,0:T(8,128)(2,1)S(1)}, bf16[64,2048]{1,0:T(8,128)(2,1)S(1)}, u32[]{:S(2)}, u32[]{:S(2)}) %collective-permute-start.2) | collective-permute-done | bytes 262176 | tf_op jit(solution)/shard_map/ppermute | solution.py:146
  23.6 0.0 collective-permute-done.3.refs_2_
  23.6 3.9 %collective-permute-done.5.refs_3_ = bf16[64,2048]{1,0:T(8,128)(2,1)S(1)} collective-permute-done((bf16[64,2048]{1,0:T(8,128)(2,1)S(1)}, bf16[64,2048]{1,0:T(8,128)(2,1)S(1)}, u32[]{:S(2)}, u32[]{:S(2)}) %collective-permute-start.5) | collective-permute-done | bytes 262176 | tf_op jit(solution)/shard_map/ppermute | solution.py:146
  27.5 1.0 %shard_map.86 = bf16[64,2048]{1,0:T(8,128)(2,1)} custom-call(f32[64,128]{1,0:T(8,128)S(1)} %shard_map.84.share_ref, bf16[64,2048]{1,0:T(8,128)(2,1)S(1)} %get-tuple-element.15.refs_0_, bf16[64,2048]{1,0:T(8,128)(2,1)S(1)} %collective-permute-done.2.refs_1_, bf16[64,2048]{1,0:T(8,128)(2,1)S(1)} %collective-permute-done.3.refs_2_, ...), custom_call_target="tpu_custom_call" | custom-call | tf_op jit(solution)/shard_map/pallas_call | solution.py:114
Async XLA Ops:
  0.0 9.9 %collective-permute-start = (bf16[64,2048]{1,0:T(8,128)(2,1)}, bf16[64,2048]{1,0:T(8,128)(2,1)S(1)}, u32[]{:S(2)}, u32[]{:S(2)}) collective-permute-start(bf16[64,2048]{1,0:T(8,128)(2,1)} %tokens_ref.3), channel_id=1, source_target_pairs={{0,2},{1,3},{2,0},{3,1},{4,6},{5,7},{6,4},{7,5},{8,10},{9,11},{10,... | collective-permute-start | bytes 786440 | tf_op jit(solution)/shard_map/ppermute | solution.py:146
  3.0 9.4 %collective-permute-start.1 = (bf16[64,2048]{1,0:T(8,128)(2,1)}, bf16[64,2048]{1,0:T(8,128)(2,1)S(1)}, u32[]{:S(2)}, u32[]{:S(2)}) collective-permute-start(bf16[64,2048]{1,0:T(8,128)(2,1)} %tokens_ref.3), channel_id=1, source_target_pairs={{0,1},{1,0},{2,3},{3,2},{4,5},{5,4},{6,7},{7,6},{8,9},{9,8},{10,11... | collective-permute-start | bytes 786440 | tf_op jit(solution)/shard_map/ppermute | solution.py:146
  4.5 13.0 %collective-permute-start.4 = (bf16[64,2048]{1,0:T(8,128)(2,1)}, bf16[64,2048]{1,0:T(8,128)(2,1)S(1)}, u32[]{:S(2)}, u32[]{:S(2)}) collective-permute-start(bf16[64,2048]{1,0:T(8,128)(2,1)} %tokens_ref.3), channel_id=1, source_target_pairs={{0,3},{1,2},{2,1},{3,0},{4,7},{5,6},{6,5},{7,4},{8,11},{9,10},{10,... | collective-permute-start | bytes 786440 | tf_op jit(solution)/shard_map/ppermute | solution.py:146
  4.5 1.0 %copy-start = (bf16[64,2048]{1,0:T(8,128)(2,1)S(1)}, bf16[64,2048]{1,0:T(8,128)(2,1)}, u32[]{:S(2)}) copy-start(bf16[64,2048]{1,0:T(8,128)(2,1)} %tokens_ref.3) | copy-start | bytes 786436
  13.9 9.8 %collective-permute-start.2 = (bf16[64,2048]{1,0:T(8,128)(2,1)S(1)}, bf16[64,2048]{1,0:T(8,128)(2,1)S(1)}, u32[]{:S(2)}, u32[]{:S(2)}) collective-permute-start(bf16[64,2048]{1,0:T(8,128)(2,1)S(1)} %get-tuple-element.16), channel_id=1, source_target_pairs={{0,1},{1,0},{2,3},{3,2},{4,5},{5,4},{6,7},{7,6},{8,9},{9,8},{10,11... | collective-permute-start | bytes 786440 | tf_op jit(solution)/shard_map/ppermute | solution.py:146
  15.5 6.8 %copy-start.1 = (bf16[64,2048]{1,0:T(8,128)(2,1)S(1)}, bf16[64,2048]{1,0:T(8,128)(2,1)}, u32[]{:S(2)}) copy-start(bf16[64,2048]{1,0:T(8,128)(2,1)} %tokens_ref.3) | copy-start | bytes 786436
  15.5 6.8 %copy-start.2 = (bf16[2048,4]{0,1:T(4,128)(2,1)S(1)}, bf16[2048,4]{0,1:T(4,128)(2,1)}, u32[]{:S(2)}) copy-start(bf16[2048,4]{0,1:T(4,128)(2,1)} %param.9) | copy-start | bytes 49156
  15.5 6.8 %copy-start.3 = (s32[64,4]{0,1:T(4,128)S(1)}, s32[64,4]{0,1:T(4,128)}, u32[]{:S(2)}) copy-start(s32[64,4]{0,1:T(4,128)} %param.13) | copy-start | bytes 3076
  15.5 6.8 %copy-start.4 = (s32[1,256]{1,0:T(1,128)S(1)}, s32[1,256]{1,0:T(1,128)}, u32[]{:S(2)}) copy-start(s32[1,256]{1,0:T(1,128)} %priority_ref.1) | copy-start | bytes 3076
  15.5 6.8 %copy-start.5 = (s32[2]{0:T(128)S(1)}, s32[2]{0:T(128)}, u32[]{:S(2)}) copy-start(s32[2]{0:T(128)} %hot_ref.1) | copy-start | bytes 28
  15.5 8.2 %collective-permute-start.3 = (bf16[64,2048]{1,0:T(8,128)(2,1)S(1)}, bf16[64,2048]{1,0:T(8,128)(2,1)S(1)}, u32[]{:S(2)}, u32[]{:S(2)}) collective-permute-start(bf16[64,2048]{1,0:T(8,128)(2,1)S(1)} %get-tuple-element.14.refs_0_), channel_id=1, source_target_pairs={{0,2},{1,3},{2,0},{3,1},{4,6},{5,7},{6,4},{7,5},{8,10},{9,11},{10,... | collective-permute-start | bytes 786440 | tf_op jit(solution)/shard_map/ppermute | solution.py:146
  19.2 8.3 %collective-permute-start.5 = (bf16[64,2048]{1,0:T(8,128)(2,1)S(1)}, bf16[64,2048]{1,0:T(8,128)(2,1)S(1)}, u32[]{:S(2)}, u32[]{:S(2)}) collective-permute-start(bf16[64,2048]{1,0:T(8,128)(2,1)S(1)} %shard_map.85), channel_id=1, source_target_pairs={{0,3},{1,2},{2,1},{3,0},{4,7},{5,6},{6,5},{7,4},{8,11},{9,10},{10,... | collective-permute-start | bytes 786440 | tf_op jit(solution)/shard_map/ppermute | solution.py:146

commit v3 on v2

--- a/solution.py
+++ b/solution.py
@@ -74,21 +74,14 @@
     )
 
 
-def first_kernel(tokens_ref, gate_in, up_in, down_in, own_ref, gate_ref, up_ref, down_ref, sems):
-    pairs = [(gate_in, gate_ref), (up_in, up_ref), (down_in, down_ref)]
-    copies = [pltpu.make_async_copy(src, dst, sems.at[i]) for i, (src, dst) in enumerate(pairs)]
+def load_kernel(*refs):
+    count = (len(refs) - 1) // 2
+    sources, targets, sems = refs[:count], refs[count : 2 * count], refs[-1]
+    copies = [pltpu.make_async_copy(src, dst, sems.at[i]) for i, (src, dst) in enumerate(zip(sources, targets))]
     for copy in copies:
         copy.start()
-
-    def landed(copy, ref):
-        def get():
-            copy.wait()
-            return ref[0]
-
-        return get
-
-    weights = [landed(copy, ref) for copy, (_, ref) in zip(copies, pairs)]
-    own_ref[...] = swiglu(tokens_ref[...], *weights).astype(own_ref.dtype)
+    for copy in copies:
+        copy.wait()
 
 
 def expert_kernel(count, *refs):
@@ -102,12 +95,25 @@
         ref[...] = result[i * step : (i + 1) * step]
 
 
-def mix_kernel(share_ref, *refs):
-    *answers, mixed_ref = refs
-    total = share_ref[:, 0:1] * answers[0][...].astype(jnp.float32)
-    for d in range(1, len(answers)):
-        total += share_ref[:, d : d + 1] * answers[d][...].astype(jnp.float32)
-    mixed_ref[...] = total.astype(mixed_ref.dtype)
+def weigh(share_ref, column, refs, total):
+    for d, ref in enumerate(refs):
+        term = share_ref[:, column + d : column + d + 1] * ref[...].astype(jnp.float32)
+        total = term if total is None else total + term
+    return total
+
+
+def gather_kernel(columns, share_ref, *refs):
+    total = None
+    for column, ref in zip(columns, refs):
+        total = weigh(share_ref, column, [ref], total)
+    refs[-1][...] = total
+
+
+def mix_kernel(columns, share_ref, total_ref, *refs):
+    total = total_ref[...]
+    for column, ref in zip(columns, refs):
+        total = weigh(share_ref, column, [ref], total)
+    refs[-1][...] = total.astype(refs[-1].dtype)
 
 
 def call(kernel, outs, operands, specs=None, scratch=(), cost=None, room=ROOM):
@@ -124,7 +130,7 @@
 
 def groups(devices_n):
     order = list(range(devices_n - 1, 0, -1))
-    return [order[:1]] + [order[i : i + 2] for i in range(1, len(order), 2)]
+    return [order[:1]] + [order[i : i + 2][::-1] for i in range(1, len(order), 2)]
 
 
 def shards(tokens, router_weight, gate_weight, up_weight, down_weight, routing, priority, hot_list):
@@ -165,29 +171,41 @@
 
     order = range(devices_n - 1, 0, -1)
     arrived = {d: send(tokens, paths[d]) for d in order}
-    own, *weights = call(
-        first_kernel,
-        (like(tokens), like(gate_weight), like(up_weight), like(down_weight)),
-        (tokens, gate_weight, up_weight, down_weight),
-        [VMEM, HBM, HBM, HBM],
-        [pltpu.SemaphoreType.DMA((3,))],
-        cost(tok_count),
-        FIRST_ROOM,
-    )
-    answers = {0: own}
+    def load(arrays):
+        size = sum(a.size for a in arrays) * 4
+        return call(
+            load_kernel,
+            [like(a) for a in arrays],
+            arrays,
+            [HBM] * len(arrays),
+            [pltpu.SemaphoreType.DMA((len(arrays),))],
+            pl.CostEstimate(flops=0, bytes_accessed=size, transcendentals=0),
+            FIRST_ROOM,
+        )
+
+    weights = load([gate_weight, up_weight, down_weight])
+    arrived[0] = tokens
+    answers = {}
     last = ()
-    for group in groups(devices_n):
+    first, *others = groups(devices_n)
+    for group in [*others, [0, *first]]:
         results = experts([arrived[d] for d in group], weights)
         last = results[:1]
         for d, result in zip(group, results):
-            answers[d] = send(result, backs[d])
+            answers[d] = send(result, backs[d]) if d else result
     share = call(
         functools.partial(share_kernel, capacity, paths),
         jax.ShapeDtypeStruct((tok_count, LANES), jnp.float32),
         (me, hot_list, tokens, router_weight.T, routing.T, priority, *last),
         [SMEM, SMEM] + [VMEM] * 4 + [ANY] * len(last),
     )
-    return call(mix_kernel, like(tokens), (share, *[answers[d] for d in range(devices_n)]))
+    late, early = first, [0, *sum(others, [])]
+    total = call(
+        functools.partial(gather_kernel, early),
+        jax.ShapeDtypeStruct(tokens.shape, jnp.float32),
+        (share, *[answers[d] for d in early]),
+    )
+    return call(functools.partial(mix_kernel, late), like(tokens), (share, total, *[answers[d] for d in late]))
 
 
 def solution(mesh):

time: 28.6 us -> 28.5 us (level)
  waiting for transfers between devices: 8.07 us -> 9.81 us
  local copies, waits for them, and re-layouts: 1.04 us -> 0.02 us
  Pallas kernels: 9.69 us -> 8.79 us
    ppermute x6, waiting for transfers between devices: 8.07 us -> 9.81 us  [send(): lax.ppermute(array, 'expert', [(i, path(i)) for i in range(devices_n)])]
    unnamed x12 -> x10, local copies, waits for them, and re-layouts: 1.04 us -> 0.02 us
    pallas_call x5 -> x6, Pallas kernels: 9.69 us -> 8.79 us  [call(): pl.pallas_call(kernel, out_shape=outs, in_specs=specs or [VMEM] * len(ope...]
  transfers between devices with their start and end apart: 6 -> 6, of which waited for: 4 -> 5; matrix products, arithmetic and copies ran while one was open for 0% -> 0% of each run, Pallas kernels for 31% -> 28%
where the time goes in v3:
time: 28.5 us; the launch traced here: 28.4 us
  waiting for transfers between devices  9.81 us (34%)
  starting transfers between devices  9.68 us (34%)
  Pallas kernels  8.79 us (31%)
    ppermute x6, waiting for transfers between devices, send(): lax.ppermute(array, 'expert', [(i, path(i)) for i in range(devices_n)])  9.81 us
    ppermute x6, starting transfers between devices, send(): lax.ppermute(array, 'expert', [(i, path(i)) for i in range(devices_n)])  9.68 us
    pallas_call x6, Pallas kernels, call(): pl.pallas_call(kernel, out_shape=outs, in_specs=specs or [VMEM] * len(ope...  8.79 us
  transfers between devices with their start and end apart: 6, of which 5 were waited for; matrix products, arithmetic and copies ran while one was open for 0% of the time, Pallas kernels for 28%

profile of v3, /device:TPU:0, one launch (start us, length us, event | category | flops | bytes accessed | tf_op | source)
XLA Modules:
  0.0 28.4 jit_solution(8697666844380336217)
XLA Ops:
  0.0 3.0 %collective-permute-start.2 = (bf16[64,2048]{1,0:T(8,128)(2,1)}, bf16[64,2048]{1,0:T(8,128)(2,1)S(1)}, u32[]{:S(2)}, u32[]{:S(2)}) collective-permute-start(bf16[64,2048]{1,0:T(8,128)(2,1)} %tokens_ref.1), channel_id=1, source_target_pairs={{0,2},{1,3},{2,0},{3,1},{4,6},{5,7},{6,4},{7,5},{8,10},{9,11},{10,... | collective-permute-start | bytes 786440 | tf_op jit(solution)/shard_map/ppermute | solution.py:152
  3.0 1.5 %collective-permute-start.1 = (bf16[64,2048]{1,0:T(8,128)(2,1)}, bf16[64,2048]{1,0:T(8,128)(2,1)S(1)}, u32[]{:S(2)}, u32[]{:S(2)}) collective-permute-start(bf16[64,2048]{1,0:T(8,128)(2,1)} %tokens_ref.1), channel_id=1, source_target_pairs={{0,1},{1,0},{2,3},{3,2},{4,5},{5,4},{6,7},{7,6},{8,9},{9,8},{10,11... | collective-permute-start | bytes 786440 | tf_op jit(solution)/shard_map/ppermute | solution.py:152
  4.5 0.0 collective-permute-start
  4.5 3.8 %shard_map.82 = (bf16[1,2048,768]{2,1,0:T(8,128)(2,1)S(1)}, bf16[1,2048,768]{2,1,0:T(8,128)(2,1)S(1)}, bf16[1,768,2048]{2,1,0:T(8,128)(2,1)S(1)}) custom-call(bf16[1,2048,768]{2,1,0:T(8,128)(2,1)} %refs_0_.2, bf16[1,2048,768]{2,1,0:T(8,128)(2,1)} %refs_1_.1, bf16[1,768,2048]{2,1,0:T(8,128)(2,1)} %refs_2_.1), custom_call_target="tpu_custom_call" | custom-call | bytes 18874368 | tf_op jit(solution)/shard_map/pallas_call | solution.py:120
  8.3 1.2 %collective-permute-done.2.refs_1_ = bf16[64,2048]{1,0:T(8,128)(2,1)S(1)} collective-permute-done((bf16[64,2048]{1,0:T(8,128)(2,1)}, bf16[64,2048]{1,0:T(8,128)(2,1)S(1)}, u32[]{:S(2)}, u32[]{:S(2)}) %collective-permute-start.2) | collective-permute-done | bytes 262176 | tf_op jit(solution)/shard_map/ppermute | solution.py:152
  9.5 2.9 %collective-permute-done.1.refs_0_ = bf16[64,2048]{1,0:T(8,128)(2,1)S(1)} collective-permute-done((bf16[64,2048]{1,0:T(8,128)(2,1)}, bf16[64,2048]{1,0:T(8,128)(2,1)S(1)}, u32[]{:S(2)}, u32[]{:S(2)}) %collective-permute-start.1) | collective-permute-done | bytes 262176 | tf_op jit(solution)/shard_map/ppermute | solution.py:152
  12.4 0.0 copy-start
  12.4 1.5 %shard_map.85 = (bf16[64,2048]{1,0:T(8,128)(2,1)S(1)}, bf16[64,2048]{1,0:T(8,128)(2,1)S(1)}) custom-call(bf16[64,2048]{1,0:T(8,128)(2,1)S(1)} %collective-permute-done.1.refs_0_, bf16[64,2048]{1,0:T(8,128)(2,1)S(1)} %collective-permute-done.2.refs_1_, bf16[1,2048,768]{2,1,0:T(8,128)(2,1)S(1)} %get-tuple-element.12.refs_2_, ...), custom_call_target="tpu_custom_call" | custom-call | flops 1207959552 | bytes 9437184 | tf_op jit(solution)/shard_map/pallas_call | solution.py:120
  13.9 1.6 %collective-permute-start.3 = (bf16[64,2048]{1,0:T(8,128)(2,1)S(1)}, bf16[64,2048]{1,0:T(8,128)(2,1)S(1)}, u32[]{:S(2)}, u32[]{:S(2)}) collective-permute-start(bf16[64,2048]{1,0:T(8,128)(2,1)S(1)} %get-tuple-element.16), channel_id=1, source_target_pairs={{0,1},{1,0},{2,3},{3,2},{4,5},{5,4},{6,7},{7,6},{8,9},{9,8},{10,11... | collective-permute-start | bytes 786440 | tf_op jit(solution)/shard_map/ppermute | solution.py:152
  15.5 0.0 copy-start.1
  15.5 0.0 copy-start.2
  15.5 0.0 copy-start.3
  15.5 0.0 copy-start.4
  15.5 0.6 %collective-permute-start.4 = (bf16[64,2048]{1,0:T(8,128)(2,1)S(1)}, bf16[64,2048]{1,0:T(8,128)(2,1)S(1)}, u32[]{:S(2)}, u32[]{:S(2)}) collective-permute-start(bf16[64,2048]{1,0:T(8,128)(2,1)S(1)} %get-tuple-element.17), channel_id=1, source_target_pairs={{0,2},{1,3},{2,0},{3,1},{4,6},{5,7},{6,4},{7,5},{8,10},{9,11},{10,... | collective-permute-start | bytes 786440 | tf_op jit(solution)/shard_map/ppermute | solution.py:152
  16.0 1.4 %collective-permute-done.refs_1_ = bf16[64,2048]{1,0:T(8,128)(2,1)S(1)} collective-permute-done((bf16[64,2048]{1,0:T(8,128)(2,1)}, bf16[64,2048]{1,0:T(8,128)(2,1)S(1)}, u32[]{:S(2)}, u32[]{:S(2)}) %collective-permute-start) | collective-permute-done | bytes 262176 | tf_op jit(solution)/shard_map/ppermute | solution.py:152
  17.4 0.0 copy-done
  17.4 1.5 %shard_map.83 = (bf16[64,2048]{1,0:T(8,128)(2,1)S(1)}, bf16[64,2048]{1,0:T(8,128)(2,1)S(1)}) custom-call(bf16[64,2048]{1,0:T(8,128)(2,1)S(1)} %copy-done, bf16[64,2048]{1,0:T(8,128)(2,1)S(1)} %collective-permute-done.refs_1_, bf16[1,2048,768]{2,1,0:T(8,128)(2,1)S(1)} %get-tuple-element.12.refs_2_, bf16[1,2048,768]{2,1,0:T(8,128)(2,1)S(1)} %get-tuple-element.13.refs_3_, ...), custom_call_target="tpu_custom_call" | custom-call | flops 1207959552 | bytes 9437184 | tf_op jit(solution)/shard_map/pallas_call | solution.py:120
  18.9 3.1 %collective-permute-start.5 = (bf16[64,2048]{1,0:T(8,128)(2,1)S(1)}, bf16[64,2048]{1,0:T(8,128)(2,1)S(1)}, u32[]{:S(2)}, u32[]{:S(2)}) collective-permute-start(bf16[64,2048]{1,0:T(8,128)(2,1)S(1)} %get-tuple-element.18), channel_id=1, source_target_pairs={{0,3},{1,2},{2,1},{3,0},{4,7},{5,6},{6,5},{7,4},{8,11},{9,10},{10,... | collective-permute-start | bytes 786440 | tf_op jit(solution)/shard_map/ppermute | solution.py:152
  22.0 0.0 copy-done.1
  22.0 0.0 copy-done.2
  22.0 0.0 copy-done.3
  22.0 0.0 copy-done.4
  22.0 1.0 %shard_map.84.share_ref = f32[64,128]{1,0:T(8,128)S(1)} custom-call(s32[1]{0:T(128)} %bitcast.me_ref, s32[2]{0:T(128)S(1)} %copy-done.4, bf16[64,2048]{1,0:T(8,128)(2,1)S(1)} %copy-done, bf16[4,2048]{1,0:T(4,128)(2,1)S(1)} %bitcast.3, s32[4,64]{1,0:T(4,128)S(1)} %bitcast.4, s32[1,256]{1,0:T(1,128)S(1)} %copy-done.3, ...), custom_call_target="tpu_custom_call" | custom-call | tf_op jit(solution)/shard_map/pallas_call | solution.py:120
  23.1 0.6 %collective-permute-done.3.refs_1_ = bf16[64,2048]{1,0:T(8,128)(2,1)S(1)} collective-permute-done((bf16[64,2048]{1,0:T(8,128)(2,1)S(1)}, bf16[64,2048]{1,0:T(8,128)(2,1)S(1)}, u32[]{:S(2)}, u32[]{:S(2)}) %collective-permute-start.3) | collective-permute-done | bytes 262176 | tf_op jit(solution)/shard_map/ppermute | solution.py:152
  23.6 0.0 collective-permute-done.4.refs_2_
  23.6 0.2 shard_map.86.total_ref
  23.9 3.7 %collective-permute-done.5.refs_0_ = bf16[64,2048]{1,0:T(8,128)(2,1)S(1)} collective-permute-done((bf16[64,2048]{1,0:T(8,128)(2,1)S(1)}, bf16[64,2048]{1,0:T(8,128)(2,1)S(1)}, u32[]{:S(2)}, u32[]{:S(2)}) %collective-permute-start.5) | collective-permute-done | bytes 262176 | tf_op jit(solution)/shard_map/ppermute | solution.py:152
  27.5 0.8 %shard_map.87 = bf16[64,2048]{1,0:T(8,128)(2,1)} custom-call(f32[64,128]{1,0:T(8,128)S(1)} %shard_map.84.share_ref, f32[64,2048]{1,0:T(8,128)S(1)} %shard_map.86.total_ref, bf16[64,2048]{1,0:T(8,128)(2,1)S(1)} %collective-permute-done.5.refs_0_), custom_call_target="tpu_custom_call" | custom-call | tf_op jit(solution)/shard_map/pallas_call | solution.py:120
Async XLA Ops:
  0.0 9.5 %collective-permute-start.2 = (bf16[64,2048]{1,0:T(8,128)(2,1)}, bf16[64,2048]{1,0:T(8,128)(2,1)S(1)}, u32[]{:S(2)}, u32[]{:S(2)}) collective-permute-start(bf16[64,2048]{1,0:T(8,128)(2,1)} %tokens_ref.1), channel_id=1, source_target_pairs={{0,2},{1,3},{2,0},{3,1},{4,6},{5,7},{6,4},{7,5},{8,10},{9,11},{10,... | collective-permute-start | bytes 786440 | tf_op jit(solution)/shard_map/ppermute | solution.py:152
  3.0 9.4 %collective-permute-start.1 = (bf16[64,2048]{1,0:T(8,128)(2,1)}, bf16[64,2048]{1,0:T(8,128)(2,1)S(1)}, u32[]{:S(2)}, u32[]{:S(2)}) collective-permute-start(bf16[64,2048]{1,0:T(8,128)(2,1)} %tokens_ref.1), channel_id=1, source_target_pairs={{0,1},{1,0},{2,3},{3,2},{4,5},{5,4},{6,7},{7,6},{8,9},{9,8},{10,11... | collective-permute-start | bytes 786440 | tf_op jit(solution)/shard_map/ppermute | solution.py:152
  4.5 13.0 %collective-permute-start = (bf16[64,2048]{1,0:T(8,128)(2,1)}, bf16[64,2048]{1,0:T(8,128)(2,1)S(1)}, u32[]{:S(2)}, u32[]{:S(2)}) collective-permute-start(bf16[64,2048]{1,0:T(8,128)(2,1)} %tokens_ref.1), channel_id=1, source_target_pairs={{0,3},{1,2},{2,1},{3,0},{4,7},{5,6},{6,5},{7,4},{8,11},{9,10},{10,... | collective-permute-start | bytes 786440 | tf_op jit(solution)/shard_map/ppermute | solution.py:152
  12.4 5.0 %copy-start = (bf16[64,2048]{1,0:T(8,128)(2,1)S(1)}, bf16[64,2048]{1,0:T(8,128)(2,1)}, u32[]{:S(2)}) copy-start(bf16[64,2048]{1,0:T(8,128)(2,1)} %tokens_ref.1) | copy-start | bytes 786436
  13.9 9.7 %collective-permute-start.3 = (bf16[64,2048]{1,0:T(8,128)(2,1)S(1)}, bf16[64,2048]{1,0:T(8,128)(2,1)S(1)}, u32[]{:S(2)}, u32[]{:S(2)}) collective-permute-start(bf16[64,2048]{1,0:T(8,128)(2,1)S(1)} %get-tuple-element.16), channel_id=1, source_target_pairs={{0,1},{1,0},{2,3},{3,2},{4,5},{5,4},{6,7},{7,6},{8,9},{9,8},{10,11... | collective-permute-start | bytes 786440 | tf_op jit(solution)/shard_map/ppermute | solution.py:152
  15.5 6.6 %copy-start.1 = (bf16[2048,4]{0,1:T(4,128)(2,1)S(1)}, bf16[2048,4]{0,1:T(4,128)(2,1)}, u32[]{:S(2)}) copy-start(bf16[2048,4]{0,1:T(4,128)(2,1)} %param.9) | copy-start | bytes 49156
  15.5 6.6 %copy-start.2 = (s32[64,4]{0,1:T(4,128)S(1)}, s32[64,4]{0,1:T(4,128)}, u32[]{:S(2)}) copy-start(s32[64,4]{0,1:T(4,128)} %param.13) | copy-start | bytes 3076
  15.5 6.6 %copy-start.3 = (s32[1,256]{1,0:T(1,128)S(1)}, s32[1,256]{1,0:T(1,128)}, u32[]{:S(2)}) copy-start(s32[1,256]{1,0:T(1,128)} %priority_ref.1) | copy-start | bytes 3076
  15.5 6.6 %copy-start.4 = (s32[2]{0:T(128)S(1)}, s32[2]{0:T(128)}, u32[]{:S(2)}) copy-start(s32[2]{0:T(128)} %hot_ref.1) | copy-start | bytes 28
  15.5 8.2 %collective-permute-start.4 = (bf16[64,2048]{1,0:T(8,128)(2,1)S(1)}, bf16[64,2048]{1,0:T(8,128)(2,1)S(1)}, u32[]{:S(2)}, u32[]{:S(2)}) collective-permute-start(bf16[64,2048]{1,0:T(8,128)(2,1)S(1)} %get-tuple-element.17), channel_id=1, source_target_pairs={{0,2},{1,3},{2,0},{3,1},{4,6},{5,7},{6,4},{7,5},{8,10},{9,11},{10,... | collective-permute-start | bytes 786440 | tf_op jit(solution)/shard_map/ppermute | solution.py:152
  18.9 8.6 %collective-permute-start.5 = (bf16[64,2048]{1,0:T(8,128)(2,1)S(1)}, bf16[64,2048]{1,0:T(8,128)(2,1)S(1)}, u32[]{:S(2)}, u32[]{:S(2)}) collective-permute-start(bf16[64,2048]{1,0:T(8,128)(2,1)S(1)} %get-tuple-element.18), channel_id=1, source_target_pairs={{0,3},{1,2},{2,1},{3,0},{4,7},{5,6},{6,5},{7,4},{8,11},{9,10},{10,... | collective-permute-start | bytes 786440 | tf_op jit(solution)/shard_map/ppermute | solution.py:152

commit v4 on v3

--- a/solution.py
+++ b/solution.py
@@ -16,7 +16,7 @@
 LANES = 128
 
 
-def kept_shares(capacity, peers, me, hot, tokens, router, routing, priority):
+def kept_shares(capacity, peers, hot, tokens, router, routing, priority):
     logits = lax.dot_general(tokens, router, (((1,), (1,)), ((), ())), preferred_element_type=jnp.float32)
     sigmas = 1.0 / (1.0 + jnp.exp(-logits))
     top, rows = routing.shape
@@ -40,8 +40,7 @@
         total += jnp.sum(jnp.where(expert_at == columns[k], sigmas, 0.0), axis=1, keepdims=True)
     lane = lax.broadcasted_iota(jnp.int32, (rows, LANES), 1)
     share = jnp.zeros((rows, LANES), jnp.float32)
-    for d, peer in enumerate(peers):
-        expert = peer(me)
+    for d, expert in enumerate(peers):
         here = jnp.zeros((rows, 1), jnp.int32)
         mine = jnp.zeros((rows, 1), jnp.int32)
         for k in range(top):
@@ -67,17 +66,17 @@
     return jnp.dot(hidden, down(), preferred_element_type=jnp.float32)
 
 
-def share_kernel(capacity, peers, me_ref, hot_ref, tokens_ref, router_ref, routing_ref, priority_ref, *refs):
+def share_kernel(capacity, peers_ref, hot_ref, tokens_ref, router_ref, routing_ref, priority_ref, *refs):
+    peers = [peers_ref[d] for d in range(peers_ref.shape[0])]
     hot = [hot_ref[h] for h in range(hot_ref.shape[0])]
     refs[-1][...] = kept_shares(
-        capacity, peers, me_ref[0], hot, tokens_ref[...], router_ref[...], routing_ref[...], priority_ref[...]
-    )
-
-
-def load_kernel(*refs):
-    count = (len(refs) - 1) // 2
-    sources, targets, sems = refs[:count], refs[count : 2 * count], refs[-1]
-    copies = [pltpu.make_async_copy(src, dst, sems.at[i]) for i, (src, dst) in enumerate(zip(sources, targets))]
+        capacity, peers, hot, tokens_ref[...], router_ref[...], routing_ref[...], priority_ref[...]
+    )
+
+
+def first_kernel(gate_in, up_in, down_in, gate_ref, up_ref, down_ref, sems):
+    pairs = [(gate_in, gate_ref), (up_in, up_ref), (down_in, down_ref)]
+    copies = [pltpu.make_async_copy(src, dst, sems.at[i]) for i, (src, dst) in enumerate(pairs)]
     for copy in copies:
         copy.start()
     for copy in copies:
@@ -128,28 +127,30 @@
     )(*operands)
 
 
-def groups(devices_n):
-    order = list(range(devices_n - 1, 0, -1))
-    return [order[:1]] + [order[i : i + 2][::-1] for i in range(1, len(order), 2)]
+def flipped(slot, devices_n):
+    bits = devices_n.bit_length() - 1
+    return sum(((slot >> b) & 1) << (bits - 1 - b) for b in range(bits))
 
 
 def shards(tokens, router_weight, gate_weight, up_weight, down_weight, routing, priority, hot_list):
-    devices_n = lax.axis_size("expert")
+    devices_n, batches_n = lax.axis_size("expert"), lax.axis_size("dp")
     tok_count, width = tokens.shape
     top_count = routing.shape[1]
     hidden_n = gate_weight.shape[2]
     slot_count = tok_count * top_count
     capacity = min(tok_count, 3 * slot_count // (2 * devices_n))
-    me = lax.axis_index("expert").astype(jnp.int32).reshape(1)
-    if devices_n & (devices_n - 1) == 0:
-        paths = [(lambda i, d=d: i ^ d) for d in range(devices_n)]
-        backs = paths
-    else:
-        paths = [(lambda i, d=d: (i + d) % devices_n) for d in range(devices_n)]
-        backs = [(lambda i, d=d: (i + devices_n - d) % devices_n) for d in range(devices_n)]
-
-    def send(array, path):
-        return lax.ppermute(array, "expert", [(i, path(i)) for i in range(devices_n)])
+    powers = devices_n & (devices_n - 1) == 0
+
+    def there(slot, batch, expert):
+        if powers:
+            return expert ^ (flipped(slot, devices_n) if batch % 2 else slot)
+        return (expert + slot) % devices_n
+
+    def send(array, slot, back=False):
+        pairs = [
+            (b * devices_n + e, b * devices_n + there(slot, b, e)) for b in range(batches_n) for e in range(devices_n)
+        ]
+        return lax.ppermute(array, ("dp", "expert"), [(d, s) for s, d in pairs] if back else pairs)
 
     def like(array):
         return jax.ShapeDtypeStruct(array.shape, array.dtype)
@@ -159,47 +160,49 @@
             flops=6 * rows * width * hidden_n, bytes_accessed=6 * width * hidden_n, transcendentals=0
         )
 
-    def experts(blocks, weights, after=()):
+    def experts(blocks, weights):
         count = len(blocks)
         return call(
             functools.partial(expert_kernel, count),
             (like(tokens),) * count,
-            (*blocks, *weights, *after),
-            [VMEM] * (count + 3) + [ANY] * len(after),
+            (*blocks, *weights),
             cost=cost(tok_count * count),
         )
 
-    order = range(devices_n - 1, 0, -1)
-    arrived = {d: send(tokens, paths[d]) for d in order}
-    def load(arrays):
-        size = sum(a.size for a in arrays) * 4
-        return call(
-            load_kernel,
-            [like(a) for a in arrays],
-            arrays,
-            [HBM] * len(arrays),
-            [pltpu.SemaphoreType.DMA((len(arrays),))],
-            pl.CostEstimate(flops=0, bytes_accessed=size, transcendentals=0),
-            FIRST_ROOM,
-        )
-
-    weights = load([gate_weight, up_weight, down_weight])
-    arrived[0] = tokens
+    me = lax.axis_index("expert").astype(jnp.int32)
+    odd = lax.axis_index("dp").astype(jnp.int32) % 2
+    tables = [
+        jnp.array([[there(slot, b, e) for slot in range(devices_n)] for e in range(devices_n)], jnp.int32) for b in (0, 1)
+    ]
+    peers = jnp.where(odd == 0, tables[0][me], tables[1][me])
+
+    arrived = {0: tokens}
+    weights = call(
+        first_kernel,
+        (like(gate_weight), like(up_weight), like(down_weight)),
+        (gate_weight, up_weight, down_weight),
+        [HBM] * 3,
+        [pltpu.SemaphoreType.DMA((3,))],
+        pl.CostEstimate(flops=0, bytes_accessed=12 * width * hidden_n, transcendentals=0),
+        FIRST_ROOM,
+    )
+    near = [slot for slot in range(1, devices_n) if not powers or slot & (slot - 1) == 0]
+    far = [slot for slot in range(1, devices_n) if slot not in near]
+    for slot in near:
+        arrived[slot] = send(tokens, slot)
+    for slot in far:
+        arrived[slot] = send(tokens, slot)
     answers = {}
-    last = ()
-    first, *others = groups(devices_n)
-    for group in [*others, [0, *first]]:
-        results = experts([arrived[d] for d in group], weights)
-        last = results[:1]
-        for d, result in zip(group, results):
-            answers[d] = send(result, backs[d]) if d else result
+    for slots in [near[i : i + 2][::-1] for i in range(0, len(near), 2)] + [([0] + far)[i : i + 2] for i in range(0, len(far) + 1, 2)]:
+        for slot, result in zip(slots, experts([arrived[slot] for slot in slots], weights)):
+            answers[slot] = send(result, slot, back=True) if slot else result
     share = call(
-        functools.partial(share_kernel, capacity, paths),
+        functools.partial(share_kernel, capacity),
         jax.ShapeDtypeStruct((tok_count, LANES), jnp.float32),
-        (me, hot_list, tokens, router_weight.T, routing.T, priority, *last),
-        [SMEM, SMEM] + [VMEM] * 4 + [ANY] * len(last),
-    )
-    late, early = first, [0, *sum(others, [])]
+        (peers, hot_list, tokens, router_weight.T, routing.T, priority, answers[0]),
+        [SMEM, SMEM] + [VMEM] * 4 + [ANY],
+    )
+    early, late = list(range(devices_n - 1)), [devices_n - 1]
     total = call(
         functools.partial(gather_kernel, early),
         jax.ShapeDtypeStruct(tokens.shape, jnp.float32),

time: 28.5 us -> 28.5 us (level)
  waiting for transfers between devices: 9.81 us -> 7.68 us
  starting transfers between devices: 9.68 us -> 11.1 us
  other arithmetic: 0 us -> 0.7 us
    ppermute x6, waiting for transfers between devices: 9.81 us -> 7.68 us  [send(): lax.ppermute(array, ('dp', 'expert'), [(d, s) for s, d in pairs] if back...]
    ppermute x6, starting transfers between devices: 9.68 us -> 11.1 us  [send(): lax.ppermute(array, ('dp', 'expert'), [(d, s) for s, d in pairs] if back...]
    select_n x0 -> x1, other arithmetic: none -> 0.7 us  [shards(): peers = jnp.where(odd == 0, tables[0][me], tables[1][me])]
  transfers between devices with their start and end apart: 6 -> 6, of which waited for: 5 -> 4; matrix products, arithmetic and copies ran while one was open for 0% -> 2% of each run, Pallas kernels for 28% -> 28%
where the time goes in v4:
time: 28.5 us; the launch traced here: 28.4 us
  starting transfers between devices  11.1 us (39%)
  Pallas kernels  8.79 us (31%)
  waiting for transfers between devices  7.68 us (27%)
  other arithmetic  0.7 us (2%)
    ppermute x6, starting transfers between devices, send(): lax.ppermute(array, ('dp', 'expert'), [(d, s) for s, d in pairs] if back...  11.1 us
    pallas_call x6, Pallas kernels, call(): pl.pallas_call(kernel, out_shape=outs, in_specs=specs or [VMEM] * len(ope...  8.79 us
    ppermute x6, waiting for transfers between devices, send(): lax.ppermute(array, ('dp', 'expert'), [(d, s) for s, d in pairs] if back...  7.68 us
    select_n x1, other arithmetic, shards(): peers = jnp.where(odd == 0, tables[0][me], tables[1][me])  0.7 us
  transfers between devices with their start and end apart: 6, of which 4 were waited for; matrix products, arithmetic and copies ran while one was open for 2% of the time, Pallas kernels for 28%

profile of v4, /device:TPU:0, one launch (start us, length us, event | category | flops | bytes accessed | tf_op | source)
XLA Modules:
  0.0 28.4 jit_solution(6958985610647097775)
XLA Ops:
  0.0 2.9 %collective-permute-start.2 = (bf16[64,2048]{1,0:T(8,128)(2,1)}, bf16[64,2048]{1,0:T(8,128)(2,1)S(1)}, u32[]{:S(2)}, u32[]{:S(2)}) collective-permute-start(bf16[64,2048]{1,0:T(8,128)(2,1)} %tokens_ref.1), channel_id=1, source_target_pairs={{0,1},{1,0},{2,3},{3,2},{4,6},{5,7},{6,4},{7,5},{8,9},{9,8},{10,11... | collective-permute-start | bytes 786440 | tf_op jit(solution)/shard_map/ppermute | solution.py:153
  2.9 1.5 %collective-permute-start.1 = (bf16[64,2048]{1,0:T(8,128)(2,1)}, bf16[64,2048]{1,0:T(8,128)(2,1)S(1)}, u32[]{:S(2)}, u32[]{:S(2)}) collective-permute-start(bf16[64,2048]{1,0:T(8,128)(2,1)} %tokens_ref.1), channel_id=1, source_target_pairs={{0,2},{1,3},{2,0},{3,1},{4,5},{5,4},{6,7},{7,6},{8,10},{9,11},{10,... | collective-permute-start | bytes 786440 | tf_op jit(solution)/shard_map/ppermute | solution.py:153
  4.5 0.0 collective-permute-start
  4.5 3.8 %shard_map.100 = (bf16[1,2048,768]{2,1,0:T(8,128)(2,1)S(1)}, bf16[1,2048,768]{2,1,0:T(8,128)(2,1)S(1)}, bf16[1,768,2048]{2,1,0:T(8,128)(2,1)S(1)}) custom-call(bf16[1,2048,768]{2,1,0:T(8,128)(2,1)} %gate_in.1, bf16[1,2048,768]{2,1,0:T(8,128)(2,1)} %up_in.1, bf16[1,768,2048]{2,1,0:T(8,128)(2,1)} %down_in.1), custom_call_target="tpu_custom_call" | custom-call | bytes 18874368 | tf_op jit(solution)/shard_map/pallas_call | solution.py:119
  8.3 1.6 %collective-permute-done.2.refs_1_ = bf16[64,2048]{1,0:T(8,128)(2,1)S(1)} collective-permute-done((bf16[64,2048]{1,0:T(8,128)(2,1)}, bf16[64,2048]{1,0:T(8,128)(2,1)S(1)}, u32[]{:S(2)}, u32[]{:S(2)}) %collective-permute-start.2) | collective-permute-done | bytes 262176 | tf_op jit(solution)/shard_map/ppermute | solution.py:153
  9.8 0.0 collective-permute-done.1.refs_0_
  9.8 0.0 copy-start
  9.9 1.5 %shard_map.103 = (bf16[64,2048]{1,0:T(8,128)(2,1)S(1)}, bf16[64,2048]{1,0:T(8,128)(2,1)S(1)}) custom-call(bf16[64,2048]{1,0:T(8,128)(2,1)S(1)} %collective-permute-done.1.refs_0_, bf16[64,2048]{1,0:T(8,128)(2,1)S(1)} %collective-permute-done.2.refs_1_, bf16[1,2048,768]{2,1,0:T(8,128)(2,1)S(1)} %get-tuple-element.12.refs_2_, ...), custom_call_target="tpu_custom_call" | custom-call | flops 1207959552 | bytes 9437184 | tf_op jit(solution)/shard_map/pallas_call | solution.py:119
  11.3 2.4 %collective-permute-start.3 = (bf16[64,2048]{1,0:T(8,128)(2,1)S(1)}, bf16[64,2048]{1,0:T(8,128)(2,1)S(1)}, u32[]{:S(2)}, u32[]{:S(2)}) collective-permute-start(bf16[64,2048]{1,0:T(8,128)(2,1)S(1)} %get-tuple-element.16), channel_id=1, source_target_pairs={{1,0},{0,1},{3,2},{2,3},{6,4},{7,5},{4,6},{5,7},{9,8},{8,9},{11,10... | collective-permute-start | bytes 786440 | tf_op jit(solution)/shard_map/ppermute | solution.py:153
  13.8 0.0 copy-start.1
  13.8 0.0 copy-start.2
  13.8 0.0 copy-start.3
  13.8 0.0 copy-start.4
  13.8 1.7 %collective-permute-start.4 = (bf16[64,2048]{1,0:T(8,128)(2,1)S(1)}, bf16[64,2048]{1,0:T(8,128)(2,1)S(1)}, u32[]{:S(2)}, u32[]{:S(2)}) collective-permute-start(bf16[64,2048]{1,0:T(8,128)(2,1)S(1)} %get-tuple-element.17), channel_id=1, source_target_pairs={{2,0},{3,1},{0,2},{1,3},{5,4},{4,5},{7,6},{6,7},{10,8},{11,9},{8,1... | collective-permute-start | bytes 786440 | tf_op jit(solution)/shard_map/ppermute | solution.py:153
  15.5 0.9 %collective-permute-done.refs_1_ = bf16[64,2048]{1,0:T(8,128)(2,1)S(1)} collective-permute-done((bf16[64,2048]{1,0:T(8,128)(2,1)}, bf16[64,2048]{1,0:T(8,128)(2,1)S(1)}, u32[]{:S(2)}, u32[]{:S(2)}) %collective-permute-start) | collective-permute-done | bytes 262176 | tf_op jit(solution)/shard_map/ppermute | solution.py:153
  16.4 0.0 copy-done
  16.4 1.5 %shard_map.101 = (bf16[64,2048]{1,0:T(8,128)(2,1)S(1)}, bf16[64,2048]{1,0:T(8,128)(2,1)S(1)}) custom-call(bf16[64,2048]{1,0:T(8,128)(2,1)S(1)} %copy-done, bf16[64,2048]{1,0:T(8,128)(2,1)S(1)} %collective-permute-done.refs_1_, bf16[1,2048,768]{2,1,0:T(8,128)(2,1)S(1)} %get-tuple-element.12.refs_2_, bf16[1,2048,768]{2,1,0:T(8,128)(2,1)S(1)} %get-tuple-element.13.refs_3_, ...), custom_call_target="tpu_custom_call" | custom-call | flops 1207959552 | bytes 9437184 | tf_op jit(solution)/shard_map/pallas_call | solution.py:119
  17.9 2.5 %collective-permute-start.5 = (bf16[64,2048]{1,0:T(8,128)(2,1)S(1)}, bf16[64,2048]{1,0:T(8,128)(2,1)S(1)}, u32[]{:S(2)}, u32[]{:S(2)}) collective-permute-start(bf16[64,2048]{1,0:T(8,128)(2,1)S(1)} %get-tuple-element.18), channel_id=1, source_target_pairs={{3,0},{2,1},{1,2},{0,3},{7,4},{6,5},{5,6},{4,7},{11,8},{10,9},{9,1... | collective-permute-start | bytes 786440 | tf_op jit(solution)/shard_map/ppermute | solution.py:153
  20.4 0.7 %fusion.peers_ref = s32[4]{0:T(128)S(1)} fusion(pred[]{:T(512)S(6)} %eq.5, s32[4,4]{1,0:T(4,128)} %constant.30.clone, s32[]{:T(128)S(6)} %select_n.23, s32[4,4]{1,0:T(4,128)} %constant.29.clone), kind=kLoop, calls=%fused_computation.1 | loop fusion | flops 4 | bytes 53 | tf_op jit(solution)/shard_map/jit(_where)/select_n | solution.py:177
  21.1 0.0 copy-done.1
  21.1 0.0 copy-done.2
  21.1 0.0 copy-done.3
  21.1 0.0 copy-done.4
  21.1 1.0 %shard_map.102.share_ref = f32[64,128]{1,0:T(8,128)S(1)} custom-call(s32[4]{0:T(128)S(1)} %fusion.peers_ref, s32[2]{0:T(128)S(1)} %copy-done.4, bf16[64,2048]{1,0:T(8,128)(2,1)S(1)} %copy-done, bf16[4,2048]{1,0:T(4,128)(2,1)S(1)} %bitcast.4, s32[4,64]{1,0:T(4,128)S(1)} %bitcast.5, s32[1,256]{1,0:T(1,128)S(1)} %copy-done.3, ...), custom_call_target="tpu_custom_call" | custom-call | tf_op jit(solution)/shard_map/pallas_call | solution.py:119
  22.1 0.0 collective-permute-done.3.refs_1_
  22.2 0.3 collective-permute-done.4.refs_2_
  22.4 0.2 shard_map.104.total_ref
  22.6 4.9 %collective-permute-done.5.refs_0_ = bf16[64,2048]{1,0:T(8,128)(2,1)S(1)} collective-permute-done((bf16[64,2048]{1,0:T(8,128)(2,1)S(1)}, bf16[64,2048]{1,0:T(8,128)(2,1)S(1)}, u32[]{:S(2)}, u32[]{:S(2)}) %collective-permute-start.5) | collective-permute-done | bytes 262176 | tf_op jit(solution)/shard_map/ppermute | solution.py:153
  27.5 0.8 %shard_map.105 = bf16[64,2048]{1,0:T(8,128)(2,1)} custom-call(f32[64,128]{1,0:T(8,128)S(1)} %shard_map.102.share_ref, f32[64,2048]{1,0:T(8,128)S(1)} %shard_map.104.total_ref, bf16[64,2048]{1,0:T(8,128)(2,1)S(1)} %collective-permute-done.5.refs_0_), custom_call_target="tpu_custom_call" | custom-call | tf_op jit(solution)/shard_map/pallas_call | solution.py:119
Async XLA Ops:
  0.0 9.8 %collective-permute-start.2 = (bf16[64,2048]{1,0:T(8,128)(2,1)}, bf16[64,2048]{1,0:T(8,128)(2,1)S(1)}, u32[]{:S(2)}, u32[]{:S(2)}) collective-permute-start(bf16[64,2048]{1,0:T(8,128)(2,1)} %tokens_ref.1), channel_id=1, source_target_pairs={{0,1},{1,0},{2,3},{3,2},{4,6},{5,7},{6,4},{7,5},{8,9},{9,8},{10,11... | collective-permute-start | bytes 786440 | tf_op jit(solution)/shard_map/ppermute | solution.py:153
  2.9 6.9 %collective-permute-start.1 = (bf16[64,2048]{1,0:T(8,128)(2,1)}, bf16[64,2048]{1,0:T(8,128)(2,1)S(1)}, u32[]{:S(2)}, u32[]{:S(2)}) collective-permute-start(bf16[64,2048]{1,0:T(8,128)(2,1)} %tokens_ref.1), channel_id=1, source_target_pairs={{0,2},{1,3},{2,0},{3,1},{4,5},{5,4},{6,7},{7,6},{8,10},{9,11},{10,... | collective-permute-start | bytes 786440 | tf_op jit(solution)/shard_map/ppermute | solution.py:153
  4.5 11.9 %collective-permute-start = (bf16[64,2048]{1,0:T(8,128)(2,1)}, bf16[64,2048]{1,0:T(8,128)(2,1)S(1)}, u32[]{:S(2)}, u32[]{:S(2)}) collective-permute-start(bf16[64,2048]{1,0:T(8,128)(2,1)} %tokens_ref.1), channel_id=1, source_target_pairs={{0,3},{1,2},{2,1},{3,0},{4,7},{5,6},{6,5},{7,4},{8,11},{9,10},{10,... | collective-permute-start | bytes 786440 | tf_op jit(solution)/shard_map/ppermute | solution.py:153
  9.8 6.5 %copy-start = (bf16[64,2048]{1,0:T(8,128)(2,1)S(1)}, bf16[64,2048]{1,0:T(8,128)(2,1)}, u32[]{:S(2)}) copy-start(bf16[64,2048]{1,0:T(8,128)(2,1)} %tokens_ref.1) | copy-start | bytes 786436
  11.3 10.8 %collective-permute-start.3 = (bf16[64,2048]{1,0:T(8,128)(2,1)S(1)}, bf16[64,2048]{1,0:T(8,128)(2,1)S(1)}, u32[]{:S(2)}, u32[]{:S(2)}) collective-permute-start(bf16[64,2048]{1,0:T(8,128)(2,1)S(1)} %get-tuple-element.16), channel_id=1, source_target_pairs={{1,0},{0,1},{3,2},{2,3},{6,4},{7,5},{4,6},{5,7},{9,8},{8,9},{11,10... | collective-permute-start | bytes 786440 | tf_op jit(solution)/shard_map/ppermute | solution.py:153
  13.8 7.3 %copy-start.1 = (bf16[2048,4]{0,1:T(4,128)(2,1)S(1)}, bf16[2048,4]{0,1:T(4,128)(2,1)}, u32[]{:S(2)}) copy-start(bf16[2048,4]{0,1:T(4,128)(2,1)} %param.11) | copy-start | bytes 49156
  13.8 7.3 %copy-start.2 = (s32[64,4]{0,1:T(4,128)S(1)}, s32[64,4]{0,1:T(4,128)}, u32[]{:S(2)}) copy-start(s32[64,4]{0,1:T(4,128)} %param.15) | copy-start | bytes 3076
  13.8 7.3 %copy-start.3 = (s32[1,256]{1,0:T(1,128)S(1)}, s32[1,256]{1,0:T(1,128)}, u32[]{:S(2)}) copy-start(s32[1,256]{1,0:T(1,128)} %priority_ref.1) | copy-start | bytes 3076
  13.8 7.3 %copy-start.4 = (s32[2]{0:T(128)S(1)}, s32[2]{0:T(128)}, u32[]{:S(2)}) copy-start(s32[2]{0:T(128)} %hot_ref.1) | copy-start | bytes 28
  13.8 8.6 %collective-permute-start.4 = (bf16[64,2048]{1,0:T(8,128)(2,1)S(1)}, bf16[64,2048]{1,0:T(8,128)(2,1)S(1)}, u32[]{:S(2)}, u32[]{:S(2)}) collective-permute-start(bf16[64,2048]{1,0:T(8,128)(2,1)S(1)} %get-tuple-element.17), channel_id=1, source_target_pairs={{2,0},{3,1},{0,2},{1,3},{5,4},{4,5},{7,6},{6,7},{10,8},{11,9},{8,1... | collective-permute-start | bytes 786440 | tf_op jit(solution)/shard_map/ppermute | solution.py:153
  17.9 9.6 %collective-permute-start.5 = (bf16[64,2048]{1,0:T(8,128)(2,1)S(1)}, bf16[64,2048]{1,0:T(8,128)(2,1)S(1)}, u32[]{:S(2)}, u32[]{:S(2)}) collective-permute-start(bf16[64,2048]{1,0:T(8,128)(2,1)S(1)} %get-tuple-element.18), channel_id=1, source_target_pairs={{3,0},{2,1},{1,2},{0,3},{7,4},{6,5},{5,6},{4,7},{11,8},{10,9},{9,1... | collective-permute-start | bytes 786440 | tf_op jit(solution)/shard_map/ppermute | solution.py:153
